TPU v7x, 32 devices: a whole 2x2x4 slice. The times are simulated.
32 devices in a mesh: row: 8 (over z, y), rep: 4 (over x, core).
Axes of the slice: x: 2, y: 2, z: 4, core: 2. Of those that a mesh axis runs over, the one named last changes fastest.
Arguments:
- feats: bfloat16 [12288, 256], P(('row', 'rep')), may hold values from -6 to 6
- weight: bfloat16 [256, 256], replicated, may hold values from -0.375 to 0.375
- bias: float32 [256], replicated, may hold values from -4 to 4
- degree: int32 [12288], P('row'), may hold values from 4 to 64
- tile_rows: int32 [8, 4, 176], P('row', 'rep'), may hold values from 0 to 11
- tile_cols: int32 [8, 4, 176], P('row', 'rep'), may hold values from 0 to 23
- tile_counts: int32 [8, 4, 176, 128, 128], P('row', 'rep'), may hold values from 0 to 3, as said below
- live_tiles: int32 [8, 4], P('row', 'rep'), may hold values from 22 to 176, as said below
- cotangent: bfloat16 [12288, 256], P(('row', 'rep')), may hold values from -6 to 6
Outputs:
- output: bfloat16 [12288, 256], P(('row', 'rep'))
- grad_feats: bfloat16 [12288, 256], P(('row', 'rep'))
- grad_weight: float32 [256, 256], replicated
- grad_bias: float32 [256], replicated
Inputs may be any that keep to these rules, and one draw needn't show every extreme that they name: A device uses its first live_tiles slots; the others are not part of the adjacency. Some device has all 176 slots in use in every draw. `tile_rows`: tile positions of a device may repeat. `tile_cols`: tile positions of a device may repeat. `tile_counts`: most entries of a tile are zero.
All inputs are finite; a program needn't handle non-finite values.
Results may differ from a plain program's by a relative error of at most 0.006.
Values may be sent and summed in bfloat16 or wider, within the bound.
No kernel may reach another device: no remote copies, remote signals or barrier semaphores. Data moves between devices by JAX's collectives and lax.ppermute only.
A program may use at most 128 MiB of HBM per device.

v0:
```python
import jax
import jax.numpy as jnp
from jax import lax
from jax.sharding import PartitionSpec as P

tiles_per_turn = 8


def tile_sum(source, target_ids, source_ids, counts, live, out_rows, transpose):
    tile_size = counts.shape[-1]
    feature_width = source.shape[1]
    turn_count = (live + tiles_per_turn - 1) // tiles_per_turn
    pattern = "gji,gjf->gif" if transpose else "gij,gjf->gif"

    def one_turn(turn_index, running):
        first = turn_index * tiles_per_turn
        sources = lax.dynamic_slice_in_dim(source_ids, first, tiles_per_turn)
        targets = lax.dynamic_slice_in_dim(target_ids, first, tiles_per_turn)
        tiles_now = lax.dynamic_slice_in_dim(counts, first, tiles_per_turn, 0).astype(jnp.bfloat16)

        def one_piece(tile_index):
            return lax.dynamic_slice_in_dim(source, tile_index * tile_size, tile_size, 0)

        pieces = jax.vmap(one_piece)(sources)
        products = jnp.einsum(pattern, tiles_now, pieces, preferred_element_type=jnp.float32)
        active = first + jnp.arange(tiles_per_turn, dtype=jnp.int32) < live
        products = jnp.where(active[:, None, None], products, jnp.zeros_like(products))
        for member in range(tiles_per_turn):
            offset = targets[member] * tile_size
            current = lax.dynamic_slice_in_dim(running, offset, tile_size, 0)
            running = lax.dynamic_update_slice_in_dim(
                running, current + products[member], offset, 0
            )
        return running

    return lax.fori_loop(0, turn_count, one_turn, jnp.zeros((out_rows, feature_width), jnp.float32))


def activation_grads(z_value, cotangent):
    sigmoid_z = jax.nn.sigmoid(z_value)
    output = (z_value * sigmoid_z).astype(jnp.bfloat16)
    grad_z = cotangent.astype(jnp.float32) * sigmoid_z * (1.0 + z_value * (1.0 - sigmoid_z))
    return (output, grad_z)


def body(feats, weight, bias, degree, tile_rows, tile_cols, tile_counts, live_tiles, cotangent):
    node_dev = feats.shape[0]
    row_nodes = degree.shape[0]
    col_nodes = node_dev * lax.axis_size("row")
    column = lax.axis_index("rep")
    row_index = lax.axis_index("row")
    row_ids = tile_rows[0, 0]
    col_ids = tile_cols[0, 0]
    counts = tile_counts[0, 0]
    live = live_tiles[0, 0]
    inv_row = lax.rsqrt(degree.astype(jnp.float32))
    inv_own = lax.dynamic_slice_in_dim(inv_row, column * node_dev, node_dev)
    scaled_q = (
        inv_own[:, None] * jnp.dot(feats, weight, preferred_element_type=jnp.float32)
    ).astype(jnp.bfloat16)
    q_columns = lax.all_gather(scaled_q, "row", axis=0, tiled=True)
    partial_value = tile_sum(q_columns, row_ids, col_ids, counts, live, row_nodes, False)
    own_slot = lax.dynamic_slice_in_dim(partial_value, column * node_dev, node_dev, 0)
    partial_value = lax.dynamic_update_slice_in_dim(
        partial_value, own_slot + scaled_q.astype(jnp.float32), column * node_dev, 0
    )
    summed = lax.psum_scatter(partial_value, "rep", scatter_dimension=0, tiled=True)
    z_own = inv_own[:, None] * summed + bias
    output, grad_own = activation_grads(z_own, cotangent)
    scaled_own = (inv_own[:, None] * grad_own).astype(jnp.bfloat16)
    scaled_rows = lax.all_gather(scaled_own, "rep", axis=0, tiled=True)
    bias_part = jnp.sum(grad_own, axis=0)
    backward = tile_sum(scaled_rows, col_ids, row_ids, counts, live, col_nodes, True)
    own_back = lax.dynamic_slice_in_dim(backward, row_index * node_dev, node_dev, 0)
    backward = lax.dynamic_update_slice_in_dim(
        backward, own_back + scaled_own.astype(jnp.float32), row_index * node_dev, 0
    )
    grad_q = lax.psum_scatter(backward, "row", scatter_dimension=0, tiled=True)
    v_full = inv_own[:, None] * grad_q
    weight_part = jnp.einsum(
        "nf,ng->fg",
        feats.astype(jnp.float32),
        v_full,
        precision=lax.Precision.HIGHEST,
        preferred_element_type=jnp.float32,
    )
    grad_weight, grad_bias = lax.psum((weight_part, bias_part), ("row", "rep"))
    v_half = v_full.astype(jnp.bfloat16)
    grad_feats = jnp.dot(v_half, weight.T, preferred_element_type=jnp.float32).astype(jnp.bfloat16)
    return (output, grad_feats, grad_weight, grad_bias)


def solution(mesh):
    return jax.shard_map(
        body,
        mesh=mesh,
        in_specs=(
            P(("row", "rep"), None),
            P(),
            P(),
            P("row"),
            P("row", "rep", None),
            P("row", "rep", None),
            P("row", "rep", None, None, None),
            P("row", "rep"),
            P(("row", "rep"), None),
        ),
        out_specs=(P(("row", "rep"), None), P(("row", "rep"), None), P(), P()),
        check_vma=False,
    )
```

profile of v0, /device:TPU:0, one launch (start us, length us, event | category | flops | bytes accessed | tf_op | source)
XLA Modules:
  0.0 1543.1 jit_solution(9252185784770462700)
XLA Ops:
  8.1 1.8 fusion.36
  10.6 47.1 %all-gather.2.cloned.1.call-done = bf16[3072,256]{1,0:T(8,128)(2,1)} async-done(((bf16[384,256]{1,0:T(8,128)(2,1)}), bf16[3072,256]{1,0:T(8,128)(2,1)}) %all-gather.2.cloned.1.call-update) | async-done | bytes 1572880 | tf_op jit(solution)/shard_map/all_gather | solution.py:61
  57.8 78.7 %while.25 = (s32[]{:T(128)}, f32[1536,256]{1,0:T(8,128)S(1)}, s32[]{:T(128)}, s32[176]{0:T(256)}, s32[]{:T(128)}, /*index=5*/s32[176,128,128]{2,1,0:T(8,128)}, s...) while((s32[]{:T(128)}, f32[1536,256]{1,0:T(8,128)S(1)}, ...), condition=%wide.region_1.2_spmd, body=%wide.region_0.1_spmd.sunk | while | flops 67764280 | bytes 5375020 | solution.py:36
  65.8 16.7 %while.28 = (s32[]{:T(128)}, bf16[3072,256]{1,0:T(8,128)(2,1)}, s32[8,2]{0,1:T(2,128)S(1)}, bf16[8,128,256]{2,1,0:T(8,128)(2,1)S(1)}, s32[]{:T(128)}) while((s32[]{:T(128)}, bf16[3072,256]{1,0:T(8,128)(2,1)}, s32[8,2]{0,1:T(2,128)S(1)}, bf16[8,128,256]{2,1,0:T(8,128)(2,1)S(1)}, s32[]{:T(128)}) %tuple.90), condition=%wide.while_cond, body=%wide.while_body.sunk | while | flops 2 | bytes 131177 | solution.py:22
  92.0 16.7 %while.28 = (s32[]{:T(128)}, bf16[3072,256]{1,0:T(8,128)(2,1)}, s32[8,2]{0,1:T(2,128)S(1)}, bf16[8,128,256]{2,1,0:T(8,128)(2,1)S(1)}, s32[]{:T(128)}) while((s32[]{:T(128)}, bf16[3072,256]{1,0:T(8,128)(2,1)}, s32[8,2]{0,1:T(2,128)S(1)}, bf16[8,128,256]{2,1,0:T(8,128)(2,1)S(1)}, s32[]{:T(128)}) %tuple.90), condition=%wide.while_cond, body=%wide.while_body.sunk | while | flops 2 | bytes 131177 | solution.py:22
  118.2 16.7 %while.28 = (s32[]{:T(128)}, bf16[3072,256]{1,0:T(8,128)(2,1)}, s32[8,2]{0,1:T(2,128)S(1)}, bf16[8,128,256]{2,1,0:T(8,128)(2,1)S(1)}, s32[]{:T(128)}) while((s32[]{:T(128)}, bf16[3072,256]{1,0:T(8,128)(2,1)}, s32[8,2]{0,1:T(2,128)S(1)}, bf16[8,128,256]{2,1,0:T(8,128)(2,1)S(1)}, s32[]{:T(128)}) %tuple.90), condition=%wide.while_cond, body=%wide.while_body.sunk | while | flops 2 | bytes 131177 | solution.py:22
  137.9 12.0 copy.13
  149.9 512.0 %reduce-scatter.3.cloned.1.call-done = f32[384,256]{1,0:T(8,128)} async-done(((f32[1536,256]{1,0:T(8,128)}), f32[384,256]{1,0:T(8,128)}) %reduce-scatter.3.cloned.1.call-update) | async-done | bytes 393232 | tf_op jit(solution)/shard_map/reduce_scatter | solution.py:67
  662.0 1.9 fusion.41
  664.0 8.6 all_gather.7
  672.9 89.3 %while.27 = (s32[]{:T(128)}, f32[3072,256]{1,0:T(8,128)S(1)}, s32[]{:T(128)}, s32[176]{0:T(256)S(1)}, s32[]{:T(128)}, /*index=5*/s32[176,128,128]{1,2,0:T(8,128)...) while((s32[]{:T(128)}, f32[3072,256]{1,0:T(8,128)S(1)}, ...), condition=%wide.region_4.5_spmd, body=%wide.region_3.4_spmd.sunk | while | flops 67764280 | bytes 5375528 | solution.py:36
  679.5 21.4 %while.29 = (s32[]{:T(128)}, bf16[1536,256]{1,0:T(8,128)(2,1)}, s32[8,2]{0,1:T(2,128)S(1)}, bf16[8,128,256]{2,1,0:T(8,128)(2,1)}, s32[]{:T(128)}) while((s32[]{:T(128)}, bf16[1536,256]{1,0:T(8,128)(2,1)}, s32[8,2]{0,1:T(2,128)S(1)}, bf16[8,128,256]{2,1,0:T(8,128)(2,1)}, s32[]{:T(128)}) %tuple.87), condition=%wide.while_cond.1, body=%wide.while_body.1.sunk | while | flops 2 | bytes 131685 | solution.py:22
  680.1 2.1 bitcast_dynamic-update-slice_fusion.4
  682.8 2.1 bitcast_dynamic-update-slice_fusion.4
  685.5 2.1 bitcast_dynamic-update-slice_fusion.4
  688.1 2.1 bitcast_dynamic-update-slice_fusion.4
  690.8 2.1 bitcast_dynamic-update-slice_fusion.4
  693.5 2.1 bitcast_dynamic-update-slice_fusion.4
  696.2 2.1 bitcast_dynamic-update-slice_fusion.4
  698.8 2.1 bitcast_dynamic-update-slice_fusion.4
  700.9 1.5 convolution_select_fusion.5
  709.3 21.4 %while.29 = (s32[]{:T(128)}, bf16[1536,256]{1,0:T(8,128)(2,1)}, s32[8,2]{0,1:T(2,128)S(1)}, bf16[8,128,256]{2,1,0:T(8,128)(2,1)}, s32[]{:T(128)}) while((s32[]{:T(128)}, bf16[1536,256]{1,0:T(8,128)(2,1)}, s32[8,2]{0,1:T(2,128)S(1)}, bf16[8,128,256]{2,1,0:T(8,128)(2,1)}, s32[]{:T(128)}) %tuple.87), condition=%wide.while_cond.1, body=%wide.while_body.1.sunk | while | flops 2 | bytes 131685 | solution.py:22
  709.9 2.1 bitcast_dynamic-update-slice_fusion.4
  712.5 2.1 bitcast_dynamic-update-slice_fusion.4
  715.2 2.1 bitcast_dynamic-update-slice_fusion.4
  717.9 2.1 bitcast_dynamic-update-slice_fusion.4
  720.6 2.1 bitcast_dynamic-update-slice_fusion.4
  723.2 2.1 bitcast_dynamic-update-slice_fusion.4
  725.9 2.1 bitcast_dynamic-update-slice_fusion.4
  728.6 2.1 bitcast_dynamic-update-slice_fusion.4
  730.7 1.5 convolution_select_fusion.5
  739.0 21.4 %while.29 = (s32[]{:T(128)}, bf16[1536,256]{1,0:T(8,128)(2,1)}, s32[8,2]{0,1:T(2,128)S(1)}, bf16[8,128,256]{2,1,0:T(8,128)(2,1)}, s32[]{:T(128)}) while((s32[]{:T(128)}, bf16[1536,256]{1,0:T(8,128)(2,1)}, s32[8,2]{0,1:T(2,128)S(1)}, bf16[8,128,256]{2,1,0:T(8,128)(2,1)}, s32[]{:T(128)}) %tuple.87), condition=%wide.while_cond.1, body=%wide.while_body.1.sunk | while | flops 2 | bytes 131685 | solution.py:22
  739.6 2.1 bitcast_dynamic-update-slice_fusion.4
  742.3 2.1 bitcast_dynamic-update-slice_fusion.4
  745.0 2.1 bitcast_dynamic-update-slice_fusion.4
  747.7 2.1 bitcast_dynamic-update-slice_fusion.4
  750.3 2.1 bitcast_dynamic-update-slice_fusion.4
  753.0 2.1 bitcast_dynamic-update-slice_fusion.4
  755.7 2.1 bitcast_dynamic-update-slice_fusion.4
  758.4 2.1 bitcast_dynamic-update-slice_fusion.4
  760.5 1.5 convolution_select_fusion.5
  763.4 1.6 copy-done.2
  765.1 603.2 %psum.15 = f32[256]{0:T(256)} all-reduce(f32[256]{0:T(256)S(1)} %get-tuple-element.168), channel_id=1, replica_groups=mesh['row'=8,'rep'=4] {'row','rep'}, use_global_device_ids=true, to_apply=%region_8.9 | all-reduce | flops 256 | bytes 2048 | tf_op jit(solution)/shard_map/psum | solution.py:87
  1368.3 35.6 %reduce-scatter.5.cloned.1.call-done = f32[384,256]{1,0:T(8,128)} async-done(((f32[3072,256]{1,0:T(8,128)}), f32[384,256]{1,0:T(8,128)}) %reduce-scatter.5.cloned.1.call-update) | async-done | bytes 393232 | tf_op jit(solution)/shard_map/reduce_scatter | solution.py:78
  1403.9 2.3 convolution_bitcast_fusion
  1406.2 1.9 convolution_convert_fusion
  1408.1 126.7 %all-reduce.4.cloned.1.call-done = f32[256,256]{0,1:T(8,128)} async-done(((f32[256,256]{0,1:T(8,128)}), f32[256,256]{0,1:T(8,128)}) %all-reduce.4.cloned.1.call-update) | async-done | bytes 262160 | tf_op jit(solution)/shard_map/psum | solution.py:87
  1534.8 1.8 copy.15
  (240 shorter events, 85.9 us)
Async XLA Ops:
  7.2 0.9 copy-start
  7.2 50.5 %all-gather.2.cloned.1.call-start = ((), (), s32[]{:S(2)}) async-start(), calls=%async_computation.2 | async-start | bytes 1769472 | tf_op jit(solution)/shard_map/all_gather | solution.py:61
  9.9 652.1 %reduce-scatter.3.cloned.1.call-start = ((), (), s32[]{:S(2)}) async-start(), calls=%async_computation.3 | async-start | bytes 1966080 | tf_op jit(solution)/shard_map/reduce_scatter | solution.py:67
  57.8 78.7 %copy-start.4 = (bf16[384,256]{1,0:T(8,128)(2,1)S(1)}, bf16[384,256]{1,0:T(8,128)(2,1)}, u32[]{:S(2)}) copy-start(bf16[384,256]{1,0:T(8,128)(2,1)} %fusion.36) | copy-start | bytes 589828
  136.6 1.2 copy-start.1
  137.9 1266.0 %reduce-scatter.5.cloned.1.call-start = ((), (), s32[]{:S(2)}) async-start(), calls=%async_computation.4 | async-start | bytes 3538944 | tf_op jit(solution)/shard_map/reduce_scatter | solution.py:78
  137.9 524.1 %copy-start.6 = (bf16[384,256]{1,0:T(8,128)(2,1)S(1)}, bf16[384,256]{1,0:T(8,128)(2,1)}, u32[]{:S(2)}) copy-start(bf16[384,256]{1,0:T(8,128)(2,1)} %param.21) | copy-start | bytes 589828
  137.9 524.0 %copy-start.7 = (f32[256]{0:T(256)S(1)}, f32[256]{0:T(256)}, u32[]{:S(2)}) copy-start(f32[256]{0:T(256)} %param.15) | copy-start | bytes 3076
  149.9 523.0 %copy-start.8 = (s32[176]{0:T(256)S(1)}, s32[176]{0:T(256)}, u32[]{:S(2)}) copy-start(s32[176]{0:T(256)} %get-tuple-element.530) | copy-start | bytes 2116
  149.9 523.0 %copy-start.9 = (s32[176]{0:T(256)S(1)}, s32[176]{0:T(256)}, u32[]{:S(2)}) copy-start(s32[176]{0:T(256)} %get-tuple-element.531) | copy-start | bytes 2116
  663.9 8.8 copy-start.3
  762.2 643.9 %copy-start.5 = (bf16[256,256]{1,0:T(8,128)(2,1)S(1)}, bf16[256,256]{1,0:T(8,128)(2,1)}, u32[]{:S(2)}) copy-start(bf16[256,256]{1,0:T(8,128)(2,1)} %param.14) | copy-start | bytes 393220
  763.4 1.6 copy-start.2
  765.1 769.7 %all-reduce.4.cloned.1.call-start = ((), (), s32[]{:S(2)}) async-start(), calls=%async_computation.5 | async-start | bytes 524288 | tf_op jit(solution)/shard_map/psum | solution.py:87
Sparse Core Ops, SparseCore 0:
  10.8 46.8 all-gather.1
  138.0 523.9 reduce-scatter.2
  765.2 638.6 reduce-scatter.4
  1410.7 124.0 all-reduce.3
where the time goes:
time: 1570 us; the launch traced here: 1540 us
  waiting for transfers between devices  721 us (46%)
  blocking collectives  612 us (39%)
  local copies, waits for them, and re-layouts  137 us (9%)
  loops' own time  31.4 us (2%)
    psum x1, blocking collectives, body(): grad_weight, grad_bias = lax.psum((weight_part, bias_part), ('row', 'rep'))  603 us
    reduce_scatter x1, waiting for transfers between devices, body(): lax.psum_scatter(partial_value, 'rep', scatter_dimension=0, tiled=True)  512 us
    psum x1, waiting for transfers between devices, body(): grad_weight, grad_bias = lax.psum((weight_part, bias_part), ('row', 'rep'))  127 us
    gather x144, local copies, waits for them, and re-layouts  114 us
    all_gather x1, waiting for transfers between devices, body(): q_columns = lax.all_gather(scaled_q, 'row', axis=0, tiled=True)  47.1 us
    reduce_scatter x1, waiting for transfers between devices, body(): grad_q = lax.psum_scatter(backward, 'row', scatter_dimension=0, tiled=True)  35.6 us
  transfers between devices with their start and end apart: 4, of which 4 were waited for; matrix products, arithmetic and copies ran while one was open for 1% of the time, Pallas kernels for 0%

commit v1 on v0

v1 whole, which is shorter than its diff:
```python
import functools

import jax
import jax.numpy as jnp
from jax import lax
from jax.experimental import pallas as pl
from jax.experimental.pallas import tpu as pltpu
from jax.sharding import PartitionSpec as P

tiles_per_turn = 8
chunk_tiles = 16
group_tiles = 4
dense_limit = 512
tail_rows = 16
f32 = jnp.float32
bf16 = jnp.bfloat16


def swap(value, axis, distance):
    size = lax.axis_size(axis)
    return lax.ppermute(value, axis, [(i, i ^ distance) for i in range(size)])


def divide(value, divisor, limit):
    factor = (1 << 16) // divisor + 1
    assert all(n * factor >> 16 == n // divisor for n in range(limit))
    return (value * factor) >> 16


def dense_kernel(
    rows_hbm, cols_hbm, live_ref, counts_ref, acc, held, exact, rows_ref, cols_ref,
    in_sems, small_sems, *, row_tiles, col_tiles, tiles_dev
):
    slots, size, _ = held.shape
    chunk = slots // in_sems.shape[0]
    half_cols = acc.shape[1]
    half_rep = row_tiles // tiles_dev // 2
    row, rep = lax.axis_index("row"), lax.axis_index("rep")

    small_copies = [
        pltpu.make_async_copy(source, target, small_sems.at[index])
        for index, (source, target) in enumerate(
            [(rows_hbm, rows_ref), (cols_hbm, cols_ref)]
        )
    ]
    for copy in small_copies:
        copy.start()

    def chunk_copy(index):
        part = pl.ds(index * chunk, chunk)
        return pltpu.make_async_copy(counts_ref.at[part], held.at[part], in_sems.at[index])

    def start_copy(index, carry):
        chunk_copy(index).start()
        return carry

    lax.fori_loop(0, slots // chunk, start_copy, 0)

    def clear(index, carry):
        part = pl.ds(pl.multiple_of(index * size, size), size)
        acc[part] = jnp.zeros((size, half_cols), bf16)
        return carry

    lax.fori_loop(0, acc.shape[0] // size, clear, 0)
    for copy in small_copies:
        copy.wait()
    live = live_ref[0, 0]

    def place(slot):
        tile_row, tile_col = rows_ref[0, 0, slot], cols_ref[0, 0, slot]
        row_owner = divide(tile_row, tiles_dev, row_tiles)
        col_owner = divide(tile_col, tiles_dev, col_tiles)
        row_place, col_place = row_owner ^ rep, col_owner ^ row
        parity = col_place & 1
        group_row = ((row_place & 1) * 2 + parity) * half_rep + (row_place >> 1)
        row_block = group_row * tiles_dev + tile_row - row_owner * tiles_dev
        col_block = (col_place >> 1) * tiles_dev + tile_col - col_owner * tiles_dev
        return row_block * size, col_block * size

    def patch(row_start, col_start):
        rows = pl.ds(pl.multiple_of(row_start, size), size)
        return acc.at[rows, pl.ds(pl.multiple_of(col_start, size), size)]

    def add_group(first, largest):
        tiles = []
        for member in range(group_tiles):
            slot = first + member
            row_start, col_start = place(slot)
            row_start = jnp.where(slot < live, row_start, acc.shape[0] - size)
            col_start = jnp.where(slot < live, col_start, 0)
            tiles.append((row_start, col_start, held[slot].astype(f32).astype(bf16)))
        for row_start, col_start, tile in tiles:
            target = patch(row_start, col_start)
            total = target[...] + tile
            target[...] = total
            for part in range(0, size, 16):
                largest = jnp.maximum(largest, total[part:part + 16])
        return largest

    def add_chunk(index, largest):
        chunk_copy(index).wait()
        first = index * chunk
        groups = jnp.clip((live - first + group_tiles - 1) // group_tiles, 0, chunk // group_tiles)
        return lax.fori_loop(
            0, groups, lambda group, so_far: add_group(first + group * group_tiles, so_far), largest
        )

    largest = lax.fori_loop(0, slots // chunk, add_chunk, jnp.zeros((16, size), bf16))

    @pl.when(jnp.max(largest.astype(f32)) >= 256.0)
    def _():
        def redo(index, carry):
            row_start = index // (col_tiles // 2) * size
            col_start = index % (col_tiles // 2) * size
            exact[...] = jnp.zeros_like(exact)

            def add_tile(slot, inner):
                at_row, at_col = place(slot)

                @pl.when((at_row == row_start) & (at_col == col_start))
                def _():
                    exact[...] += held[slot]

                return inner

            lax.fori_loop(0, live, add_tile, 0)
            patch(row_start, col_start)[...] = exact[...].astype(f32).astype(bf16)
            return carry

        lax.fori_loop(0, row_tiles * col_tiles, redo, 0)


def dense_adjacency(tile_rows, tile_cols, live_tiles, counts, row_tiles, col_tiles, tiles_dev):
    slots, size, _ = counts.shape
    shape = ((2 * row_tiles + 1) * size, col_tiles // 2 * size)
    in_hbm = pl.BlockSpec(memory_space=pltpu.HBM)
    tile_rows, tile_cols, counts = [
        pltpu.with_memory_space_constraint(value, pltpu.HBM)
        for value in (tile_rows, tile_cols, counts)
    ]
    return pl.pallas_call(
        functools.partial(
            dense_kernel, row_tiles=row_tiles, col_tiles=col_tiles, tiles_dev=tiles_dev
        ),
        out_shape=pltpu.VMEM(shape, bf16),
        in_specs=[in_hbm, in_hbm, pl.BlockSpec(memory_space=pltpu.SMEM), in_hbm],
        out_specs=pl.BlockSpec(memory_space=pltpu.VMEM),
        scratch_shapes=[
            pltpu.VMEM(counts.shape, jnp.int32),
            pltpu.VMEM((size, size), jnp.int32),
            pltpu.SMEM(tile_rows.shape, jnp.int32),
            pltpu.SMEM(tile_cols.shape, jnp.int32),
            pltpu.SemaphoreType.DMA((slots // chunk_tiles,)),
            pltpu.SemaphoreType.DMA((2,)),
        ],
        compiler_params=pltpu.CompilerParams(
            vmem_limit_bytes=4 * counts.size + (3 << 20)
        ),
        cost_estimate=pl.CostEstimate(
            flops=shape[0] * shape[1], bytes_accessed=4 * counts.size, transcendentals=0
        ),
        name="dense_adjacency",
    )(tile_rows, tile_cols, live_tiles, counts)


def tile_sum(source, target_ids, source_ids, counts, live, out_rows, transpose):
    tile_size = counts.shape[-1]
    feature_width = source.shape[1]
    turn_count = (live + tiles_per_turn - 1) // tiles_per_turn
    pattern = "gji,gjf->gif" if transpose else "gij,gjf->gif"

    def one_turn(turn_index, running):
        first = turn_index * tiles_per_turn
        sources = lax.dynamic_slice_in_dim(source_ids, first, tiles_per_turn)
        targets = lax.dynamic_slice_in_dim(target_ids, first, tiles_per_turn)
        tiles_now = lax.dynamic_slice_in_dim(counts, first, tiles_per_turn, 0).astype(bf16)

        def one_piece(tile_index):
            return lax.dynamic_slice_in_dim(source, tile_index * tile_size, tile_size, 0)

        pieces = jax.vmap(one_piece)(sources)
        products = jnp.einsum(pattern, tiles_now, pieces, preferred_element_type=f32)
        active = first + jnp.arange(tiles_per_turn, dtype=jnp.int32) < live
        products = jnp.where(active[:, None, None], products, jnp.zeros_like(products))
        for member in range(tiles_per_turn):
            offset = targets[member] * tile_size
            current = lax.dynamic_slice_in_dim(running, offset, tile_size, 0)
            running = lax.dynamic_update_slice_in_dim(
                running, current + products[member], offset, 0
            )
        return running

    return lax.fori_loop(0, turn_count, one_turn, jnp.zeros((out_rows, feature_width), f32))


def after(value, *earlier):
    return lax.optimization_barrier((value, earlier))[0]


def gather_row(value, ready, others):
    size = lax.axis_size("row")
    pieces = {0: value}
    bit = size // 2
    while bit > 1:
        arrived = swap(value, "row", bit)
        pieces[bit] = after(arrived, *ready)
        ready = [*ready, arrived]
        bit //= 2
    singles = [pieces[place] for place in sorted(pieces) if place] + others
    bit = size // 2
    while bit > 1:
        for place in range(2 * bit, size, 2 * bit):
            pieces[place + bit] = swap(after(pieces[place], *singles), "row", bit)
        bit //= 2
    for place in range(0, size, 2):
        if place != 2:
            source = after(pieces[place], *singles) if place < size - 2 and place else pieces[place]
            pieces[place + 1] = swap(source, "row", 1)
    if size > 2:
        pieces[3] = swap(after(pieces[1], pieces[size - 2]), "row", 2)
    for place in range(5, size - 1, 2):
        pieces[place] = after(pieces[place], pieces[size - 2])
    return pieces


def pair_rows(bias_row):
    high = bias_row.astype(bf16).astype(f32)
    index = lax.broadcasted_iota(jnp.int32, (tail_rows, bias_row.shape[1]), 0)
    return jnp.where(index == 0, high, jnp.where(index == 1, bias_row - high, 0.0))


def message_kernel(*refs, width_rows):
    block_refs, (own_ref, moved_ref, out_ref) = refs[:-3], refs[-3:]
    nodes = out_ref.shape[0] - width_rows
    if nodes:
        total = block_refs[0][...]
        for ref in block_refs[1:]:
            total = total + ref[:nodes].astype(f32)
        out_ref[:nodes] = total.astype(out_ref.dtype)
    own = own_ref[own_ref.shape[0] - width_rows:].astype(f32)
    values = own + moved_ref[moved_ref.shape[0] - width_rows:].astype(f32)
    main = width_rows - tail_rows
    bias_row = values[main:main + 1] + values[main + 1:main + 2]
    out_ref[nodes:nodes + main] = values[:main].astype(out_ref.dtype)
    out_ref[nodes + main:] = pair_rows(bias_row).astype(out_ref.dtype)


def build_message(blocks, own, moved, width_rows, dtype=bf16):
    nodes = blocks[0].shape[0] if blocks else 0
    width = own.shape[1]
    whole = pl.BlockSpec(memory_space=pltpu.VMEM)
    return pl.pallas_call(
        functools.partial(message_kernel, width_rows=width_rows),
        out_shape=jax.ShapeDtypeStruct((nodes + width_rows, width), dtype),
        in_specs=[whole] * (len(blocks) + 2),
        out_specs=whole,
        compiler_params=pltpu.CompilerParams(vmem_limit_bytes=8 << 20),
        cost_estimate=pl.CostEstimate(
            flops=nodes * width, bytes_accessed=8 * nodes * width, transcendentals=0
        ),
        name="build_message",
    )(*blocks, own, moved)


def reduce_row(block, own, start_payload):
    def message(value, *earlier):
        return after(value.astype(bf16), *earlier)

    nodes = own.shape[0]
    payload, begun = start_payload(own)
    width_rows = payload.shape[0]
    far7 = message(block(7, begun))
    moved7 = swap(far7, "row", 2)
    rows_moved = swap(payload, "row", 4)
    far3 = message(block(3, far7))
    moved3 = swap(far3, "row", 1)
    near6 = block(6, far3)
    far5 = block(5, near6)
    sent6 = build_message([near6], payload, rows_moved, width_rows)
    moved6 = swap(sent6, "row", 2)
    moved5 = swap(message(far5 + moved7.astype(f32), moved3), "row", 1)
    near4 = block(4, sent6)
    near4 = message(near4 + moved5.astype(f32) + moved6[:nodes].astype(f32))
    moved4 = swap(near4, "row", 4)
    near2 = message(block(2, sent6) + moved3.astype(f32))
    moved2 = swap(near2, "row", 2)
    sent1 = build_message([block(1, near4)], sent6, moved6, width_rows)
    moved1 = swap(sent1, "row", 1)
    payload = build_message([], sent1, moved1, width_rows)
    total = block(0, near2) + own.astype(f32) + moved2.astype(f32) + moved1[:nodes].astype(f32)
    return total + moved4.astype(f32), payload


def reduce_row_plainly(block, own, start_payload):
    size = lax.axis_size("row")
    sums = {place: block(place) for place in range(size)}
    sums[0] = sums[0] + own.astype(f32)
    payload, _ = start_payload(sums[size - 1].astype(bf16))
    bit = 1
    while bit < size:
        for place in sorted(sums, reverse=True):
            if place & bit:
                moved = swap(sums.pop(place).astype(bf16), "row", bit)
                sums[place - bit] = sums[place - bit] + moved.astype(f32)
        payload = build_message([], payload, swap(payload, "row", bit), payload.shape[0])
        bit *= 2
    return sums[0], payload


def reduce_rep(sums):
    sums = dict(sums)
    bit = 1
    while bit < lax.axis_size("rep"):
        for place in sorted(sums, reverse=True):
            if place & bit:
                moved = swap(sums.pop(place).astype(bf16), "rep", bit)
                sums[place - bit] = sums[place - bit] + moved.astype(f32)
        bit *= 2
    return sums[0]


def weight_kernel(*refs, parts, distances):
    summed_refs, scaled_refs, grad_refs = refs[:parts], refs[parts:2 * parts], refs[2 * parts:3 * parts]
    out_ref, whole = refs[-2:]
    rows = out_ref.shape[1] - tail_rows
    rep = lax.axis_index("rep")
    weight_part, bias_row = 0.0, 0.0
    for summed_ref, scaled_ref, grad_ref in zip(summed_refs, scaled_refs, grad_refs):
        weight_part += lax.dot_general(
            summed_ref[...], scaled_ref[...].astype(f32), (((0,), (0,)), ((), ())),
            precision=lax.Precision.HIGHEST, preferred_element_type=f32,
        )
        bias_row += jnp.sum(grad_ref[...], axis=0, keepdims=True)
    whole[...] = weight_part
    for index, distance in enumerate(distances):
        start = pl.multiple_of((rep ^ distance) * rows, rows)
        out_ref[index, :rows] = whole[pl.ds(start, rows)]
        out_ref[index, rows:] = pair_rows(bias_row)


def weight_blocks(summed, scaled, grads, earlier, n_rep, distances):
    nodes, width = summed[0].shape
    parts = len(summed)
    whole = pl.BlockSpec(memory_space=pltpu.VMEM)
    return pl.pallas_call(
        functools.partial(weight_kernel, parts=parts, distances=distances),
        out_shape=jax.ShapeDtypeStruct((len(distances), width // n_rep + tail_rows, width), f32),
        in_specs=[whole] * (3 * parts) + [pl.BlockSpec(memory_space=pl.ANY)],
        out_specs=whole,
        scratch_shapes=[pltpu.VMEM((width, width), f32)],
        compiler_params=pltpu.CompilerParams(vmem_limit_bytes=8 << 20),
        cost_estimate=pl.CostEstimate(
            flops=12 * parts * nodes * width * width,
            bytes_accessed=16 * parts * nodes * width,
            transcendentals=0,
        ),
        name="weight_blocks",
    )(*summed, *scaled, *grads, earlier)


def join_kernel(*refs):
    part_refs, (out_ref, bias_ref) = refs[:-2], refs[-2:]
    rows = out_ref.shape[0] // len(part_refs)
    rep = lax.axis_index("rep")
    bias_row = jnp.zeros_like(bias_ref)
    for distance, ref in enumerate(part_refs):
        values = ref[...].astype(f32)
        out_ref[pl.ds(pl.multiple_of((rep ^ distance) * rows, rows), rows)] = values[:rows]
        bias_row = jnp.where(rep == distance, values[rows:rows + 1] + values[rows + 1:rows + 2], bias_row)
    bias_ref[...] = bias_row


def weight_part(blocks, distances):
    total = blocks[0]
    for index, distance in enumerate(distances):
        if distance:
            total = build_message([], total, swap(blocks[index], "rep", distance), total.shape[0], f32)
    return total


def weight_join(total, n_rep, earlier):
    rows, width = total.shape
    rows -= tail_rows
    parts = [total]
    parts += [after(swap(total, "rep", distance), earlier) for distance in range(1, n_rep)]
    whole = pl.BlockSpec(memory_space=pltpu.VMEM)
    grad_weight, grad_bias = pl.pallas_call(
        join_kernel,
        out_shape=[
            jax.ShapeDtypeStruct((n_rep * rows, width), f32),
            jax.ShapeDtypeStruct((1, width), f32),
        ],
        in_specs=[whole] * n_rep,
        out_specs=[whole] * 2,
        compiler_params=pltpu.CompilerParams(vmem_limit_bytes=4 << 20),
        cost_estimate=pl.CostEstimate(
            flops=n_rep * rows * width, bytes_accessed=8 * n_rep * rows * width, transcendentals=0
        ),
        name="join_blocks",
    )(*parts)
    return grad_weight, grad_bias.reshape(width)


def body(feats, weight, bias, degree, tile_rows, tile_cols, tile_counts, live_tiles, cotangent):
    node_dev, width = feats.shape
    n_row, n_rep = lax.axis_size("row"), lax.axis_size("rep")
    row, rep = lax.axis_index("row"), lax.axis_index("rep")
    counts = tile_counts[0, 0]
    size = counts.shape[-1]
    tiles_dev = node_dev // size
    row_tiles, col_tiles = tiles_dev * n_rep, tiles_dev * n_row
    half_row, half_rep = n_row // 2, n_rep // 2

    paired = n_rep == 4
    places = (0, 2) if paired else (0,)

    inv_row = lax.rsqrt(degree.astype(f32))
    inv = {
        place: lax.dynamic_slice_in_dim(inv_row, (rep ^ place) * node_dev, node_dev)[:, None]
        for place in places
    }
    inv_own = inv[0]
    cotangents = {0: cotangent}
    if paired:
        cotangents[2] = swap(cotangent, "rep", 2)

    dense = row_tiles * col_tiles <= dense_limit
    if dense:
        adjacency = dense_adjacency(
            after(tile_rows, *inv.values()), tile_cols, live_tiles, counts,
            row_tiles, col_tiles, tiles_dev,
        )
    else:
        live = live_tiles[0, 0]
        row_ids = ((tile_rows[0, 0] // tiles_dev) ^ rep) * tiles_dev + tile_rows[0, 0] % tiles_dev
        col_place = (tile_cols[0, 0] // tiles_dev) ^ row
        col_place = col_place // 2 + col_place % 2 * half_row
        col_ids = col_place * tiles_dev + tile_cols[0, 0] % tiles_dev

    scaled_x = (inv_own * feats.astype(f32)).astype(bf16)

    pieces = gather_row(scaled_x, [adjacency] if dense else (), [cotangents[2]] if paired else [])
    even = jnp.concatenate([pieces[place] for place in range(0, n_row, 2)])
    odd = jnp.concatenate([pieces[place] for place in range(1, n_row - 1, 2)])

    if dense:
        def block(place, parity, count=1):
            first = ((place % 2 * 2 + parity) * half_rep + place // 2) * node_dev
            return adjacency[first:first + count * node_dev]

        def aggregate(place):
            most = (half_row - 1) * node_dev
            even_cols, odd_cols = block(place, 0, half_rep), block(place, 1, half_rep)
            before = jnp.dot(even_cols, even, preferred_element_type=f32)
            before = before + jnp.dot(odd_cols[:, :most], odd, preferred_element_type=f32)
            return before + jnp.dot(odd_cols[:, most:], pieces[n_row - 1], preferred_element_type=f32)

        near_sum, far_sum = aggregate(0), aggregate(1)
    else:
        sums = tile_sum(
            jnp.concatenate([even, odd, pieces[n_row - 1]]), row_ids, col_ids, counts, live,
            row_tiles * size, False,
        ).reshape(half_rep, 2, node_dev, width)
        near_sum, far_sum = sums[:, 0].reshape(-1, width), sums[:, 1].reshape(-1, width)
    near_sum = near_sum + swap(far_sum.astype(bf16), "rep", 1).astype(f32)
    near_sum = near_sum + jnp.pad(
        scaled_x.astype(f32), ((0, near_sum.shape[0] - node_dev), (0, 0))
    )
    if paired:
        other = swap(near_sum.astype(bf16), "rep", 2)
        summed = {
            0: near_sum[:node_dev] + other[node_dev:].astype(f32),
            2: near_sum[node_dev:] + other[:node_dev].astype(f32),
        }
    else:
        near_sum = near_sum.reshape(half_rep, node_dev, width)
        summed = {0: reduce_rep({2 * place: near_sum[place] for place in range(half_rep)})}

    def activate(place):
        z = inv[place] * jnp.dot(
            summed[place], weight.astype(f32),
            precision=lax.Precision.HIGHEST, preferred_element_type=f32,
        ) + bias
        sigmoid_z = jax.nn.sigmoid(z)
        grad_z = cotangents[place].astype(f32) * sigmoid_z * (1.0 + z * (1.0 - sigmoid_z))
        return (z * sigmoid_z).astype(bf16), grad_z, (inv[place] * grad_z).astype(bf16)

    outputs, grads, received = {}, {}, {}
    for place in places:
        outputs[place], grads[place], received[place] = activate(place)
    output, scaled_r = outputs[0], received[0]
    for bit in reversed(range(n_rep.bit_length() - 1)):
        for place in sorted(received):
            if place + (1 << bit) < n_rep and not place % (2 << bit) and place + (1 << bit) not in received:
                received[place + (1 << bit)] = swap(received[place], "rep", 1 << bit)

    def transposed(matrix, value):
        return lax.dot_general(matrix, value, (((0,), (0,)), ((), ())), preferred_element_type=f32)

    if dense:
        begun = {}
        late = [place for place in range(1, n_rep, 2)]

        def back_block(index, *earlier):
            parity = index % 2
            if parity not in begun:
                begun[parity] = 0.0
                for place in range(0, n_rep, 2):
                    value = after(received[place], *earlier)
                    begun[parity] = begun[parity] + transposed(block(place, parity), value)
            part = slice(index // 2 * node_dev, (index // 2 + 1) * node_dev)
            total = begun[parity][part]
            for place in late:
                value = after(received[place], received[late[-1]], *earlier)
                total = total + transposed(block(place, parity)[:, part], value)
            return total
    else:
        backward = tile_sum(
            jnp.concatenate([received[place] for place in range(n_rep)]),
            col_ids, row_ids, counts, live, col_tiles * size, True,
        ).reshape(n_row, node_dev, width)

        def back_block(index, *earlier):
            return backward[index // 2 + index % 2 * half_row]

    def start_payload(earlier):
        distances = (0, 1) if paired else tuple(range(n_rep))
        blocks = weight_blocks(
            [summed[place] for place in places], [received[place] for place in places],
            [grads[place] for place in places], earlier, n_rep, distances,
        )
        return weight_part(blocks, distances), blocks

    reduce_over_row = reduce_row if n_row == 8 else reduce_row_plainly
    grad_q, weight_total = reduce_over_row(back_block, scaled_r, start_payload)
    v_half = after((inv_own * grad_q).astype(bf16))
    grad_feats = jnp.dot(v_half, weight.T, preferred_element_type=f32).astype(bf16)
    grad_weight, grad_bias = weight_join(weight_total, n_rep, grad_feats)
    return (output, grad_feats, grad_weight, grad_bias)


def solution(mesh):
    return jax.shard_map(
        body,
        mesh=mesh,
        in_specs=(
            P(("row", "rep"), None),
            P(),
            P(),
            P("row"),
            P("row", "rep", None),
            P("row", "rep", None),
            P("row", "rep", None, None, None),
            P("row", "rep"),
            P(("row", "rep"), None),
        ),
        out_specs=(P(("row", "rep"), None), P(("row", "rep"), None), P(), P()),
        check_vma=False,
    )
```

time: 1570 us -> 81.3 us (0.05); the launches traced: 1540 us -> 81.1 us
  waiting for transfers between devices: 721 us -> 26.8 us
  blocking collectives: 612 us -> 0 us
  local copies, waits for them, and re-layouts: 137 us -> 0.16 us
  loops' own time: 31.4 us -> 0 us
  starting transfers between devices: 0.16 us -> 30.6 us
    psum x1 -> x0, blocking collectives: 603 us -> none  [body(): grad_weight, grad_bias = lax.psum((weight_part, bias_part), ('row', 'rep'))]
    reduce_scatter x2 -> x0, waiting for transfers between devices: 548 us -> none  [the longest x1 512 us: body(): lax.psum_scatter(partial_value, 'rep', scatter_dimension=0, tiled=True)]
    psum x1 -> x0, waiting for transfers between devices: 127 us -> none  [body(): grad_weight, grad_bias = lax.psum((weight_part, bias_part), ('row', 'rep'))]
    gather x144 -> x0, local copies, waits for them, and re-layouts: 114 us -> none
    all_gather x1 -> x0, waiting for transfers between devices: 47.1 us -> none  [body(): q_columns = lax.all_gather(scaled_q, 'row', axis=0, tiled=True)]
    another operation x8 -> x0, loops' own time: 31.4 us -> none  [the longest x2 30.9 us: tile_sum(): lax.fori_loop(0, turn_count, one_turn, jnp.zeros((out_rows, feature_width...]
    ppermute x0 -> x24, starting transfers between devices: none -> 30.6 us  [swap(): return lax.ppermute(value, axis, [(i, i ^ distance) for i in range(size)])]
    ppermute x0 -> x24, waiting for transfers between devices: none -> 26.8 us  [swap(): return lax.ppermute(value, axis, [(i, i ^ distance) for i in range(size)])]
  transfers between devices with their start and end apart: 4 -> 24, of which waited for: 4 -> 11; matrix products, arithmetic and copies ran while one was open for 1% -> 14% of each run, Pallas kernels for 0% -> 6%
where the time goes in v1:
time: 81.3 us; the launch traced here: 81.1 us
  starting transfers between devices  30.6 us (38%)
  waiting for transfers between devices  26.8 us (33%)
  matrix products  13.5 us (17%)
  Pallas kernels  6.5 us (8%)
  other arithmetic  1.86 us (2%)
  between operations  1.68 us (2%)
    ppermute x24, starting transfers between devices, swap(): return lax.ppermute(value, axis, [(i, i ^ distance) for i in range(size)])  30.6 us
    ppermute x24, waiting for transfers between devices, swap(): return lax.ppermute(value, axis, [(i, i ^ distance) for i in range(size)])  26.8 us
    dot_general x20, matrix products, transposed(): lax.dot_general(matrix, value, (((0,), (0,)), ((), ())), preferred_elemen...  7.34 us
    pallas_call x1, Pallas kernels, dense_adjacency(): pl.pallas_call(functools.partial(dense_kernel, row_tiles=row_tiles, col_t...  4.57 us
  transfers between devices with their start and end apart: 24, of which 11 were waited for; matrix products, arithmetic and copies ran while one was open for 14% of the time, Pallas kernels for 6%

profile of v1, /device:TPU:0, one launch (start us, length us, event | category | flops | bytes accessed | tf_op | source)
XLA Modules:
  0.0 81.1 jit_solution(12686744643506314080)
XLA Ops:
  0.7 0.7 convert_rsqrt_fusion
  1.5 1.0 %multiply_convert_fusion.3 = bf16[384,256]{1,0:T(8,128)(2,1)S(1)} fusion(bf16[384,256]{1,0:T(8,128)(2,1)} %param.9, f32[384]{0:T(512)S(1)} %get-tuple-element.70), kind=kLoop, calls=%fused_computation.70 | loop fusion | flops 294912 | bytes 394752 | tf_op jit(solution)/shard_map/convert_element_type | solution.py:440
  2.5 4.1 %collective-permute-start.1 = (bf16[384,256]{1,0:T(8,128)(2,1)S(1)}, bf16[384,256]{1,0:T(8,128)(2,1)S(1)}, u32[]{:S(2)}, u32[]{:S(2)}) collective-permute-start(bf16[384,256]{1,0:T(8,128)(2,1)S(1)} %multiply_convert_fusion.3), channel_id=1, source_target_pairs={{0,16},{4,20},{8,24},{12,28},{16,0},{20,4},{24,8},{28,12},{1,17},{... | collective-permute-start | bytes 589832 | tf_op jit(solution)/shard_map/ppermute | solution.py:21
  6.6 1.6 %collective-permute-start = (bf16[384,256]{1,0:T(8,128)(2,1)S(1)}, bf16[384,256]{1,0:T(8,128)(2,1)S(1)}, u32[]{:S(2)}, u32[]{:S(2)}) collective-permute-start(bf16[384,256]{1,0:T(8,128)(2,1)S(1)} %multiply_convert_fusion.3), channel_id=1, source_target_pairs={{0,8},{4,12},{8,0},{12,4},{16,24},{20,28},{24,16},{28,20},{1,9},{5... | collective-permute-start | bytes 589832 | tf_op jit(solution)/shard_map/ppermute | solution.py:21
  8.2 1.5 %collective-permute-start.2 = (bf16[384,256]{1,0:T(8,128)(2,1)}, bf16[384,256]{1,0:T(8,128)(2,1)S(1)}, u32[]{:S(2)}, u32[]{:S(2)}) collective-permute-start(bf16[384,256]{1,0:T(8,128)(2,1)} %param.17), channel_id=1, source_target_pairs={{0,2},{1,3},{2,0},{3,1},{4,6},{5,7},{6,4},{7,5},{8,10},{9,11},{10,... | collective-permute-start | bytes 589832 | tf_op jit(solution)/shard_map/ppermute | solution.py:21
  9.7 1.5 %collective-permute-start.4 = (bf16[384,256]{1,0:T(8,128)(2,1)S(1)}, bf16[384,256]{1,0:T(8,128)(2,1)S(1)}, u32[]{:S(2)}, u32[]{:S(2)}) collective-permute-start(bf16[384,256]{1,0:T(8,128)(2,1)S(1)} %multiply_convert_fusion.3), channel_id=1, source_target_pairs={{0,4},{4,0},{8,12},{12,8},{16,20},{20,16},{24,28},{28,24},{1,5},{5... | collective-permute-start | bytes 589832 | tf_op jit(solution)/shard_map/ppermute | solution.py:21
  11.9 4.6 %dense_adjacency.1 = bf16[3200,1536]{1,0:T(8,128)(2,1)S(1)} custom-call(s32[1,1,176]{2,1,0:T(1,128)} %rows_hbm, s32[1,1,176]{2,1,0:T(1,128)} %cols_hbm.1, s32[1,1]{1,0:T(1,128)S(6)} %copy.15.live_ref, s32[176,128,128]{2,1,0:T(8,128)} %bitcast.36), custom_call_target="tpu_custom_call" | custom-call | flops 4915200 | bytes 11534336 | tf_op jit(solution)/shard_map/dense_adjacency/pallas_call | solution.py:141
  16.5 1.1 %collective-permute-start.3 = (bf16[384,256]{1,0:T(8,128)(2,1)S(1)}, bf16[384,256]{1,0:T(8,128)(2,1)S(1)}, u32[]{:S(2)}, u32[]{:S(2)}) collective-permute-start(bf16[384,256]{1,0:T(8,128)(2,1)S(1)} %collective-permute-done.1), channel_id=1, source_target_pairs={{0,8},{4,12},{8,0},{12,4},{16,24},{20,28},{24,16},{28,20},{1,9},{5... | collective-permute-start | bytes 589832 | tf_op jit(solution)/shard_map/ppermute | solution.py:21
  17.5 1.5 %collective-permute-start.6 = (bf16[384,256]{1,0:T(8,128)(2,1)S(1)}, bf16[384,256]{1,0:T(8,128)(2,1)S(1)}, u32[]{:S(2)}, u32[]{:S(2)}) collective-permute-start(bf16[384,256]{1,0:T(8,128)(2,1)S(1)} %collective-permute-done.1), channel_id=1, source_target_pairs={{0,4},{4,0},{8,12},{12,8},{16,20},{20,16},{24,28},{28,24},{1,5},{5... | collective-permute-start | bytes 589832 | tf_op jit(solution)/shard_map/ppermute | solution.py:21
  19.1 3.2 %collective-permute-done.3 = bf16[384,256]{1,0:T(8,128)(2,1)S(1)} collective-permute-done((bf16[384,256]{1,0:T(8,128)(2,1)S(1)}, bf16[384,256]{1,0:T(8,128)(2,1)S(1)}, u32[]{:S(2)}, u32[]{:S(2)}) %collective-permute-start.3) | collective-permute-done | bytes 196640 | tf_op jit(solution)/shard_map/ppermute | solution.py:21
  22.2 1.1 %collective-permute-start.5 = (bf16[384,256]{1,0:T(8,128)(2,1)S(1)}, bf16[384,256]{1,0:T(8,128)(2,1)S(1)}, u32[]{:S(2)}, u32[]{:S(2)}) collective-permute-start(bf16[384,256]{1,0:T(8,128)(2,1)S(1)} %collective-permute-done.4), channel_id=1, source_target_pairs={{0,8},{4,12},{8,0},{12,4},{16,24},{20,28},{24,16},{28,20},{1,9},{5... | collective-permute-start | bytes 589832 | tf_op jit(solution)/shard_map/ppermute | solution.py:21
  23.3 1.6 %collective-permute-start.7 = (bf16[384,256]{1,0:T(8,128)(2,1)S(1)}, bf16[384,256]{1,0:T(8,128)(2,1)S(1)}, u32[]{:S(2)}, u32[]{:S(2)}) collective-permute-start(bf16[384,256]{1,0:T(8,128)(2,1)S(1)} %collective-permute-done.3), channel_id=1, source_target_pairs={{0,4},{4,0},{8,12},{12,8},{16,20},{20,16},{24,28},{28,24},{1,5},{5... | collective-permute-start | bytes 589832 | tf_op jit(solution)/shard_map/ppermute | solution.py:21
  24.9 3.0 %collective-permute-done.5 = bf16[384,256]{1,0:T(8,128)(2,1)S(1)} collective-permute-done((bf16[384,256]{1,0:T(8,128)(2,1)S(1)}, bf16[384,256]{1,0:T(8,128)(2,1)S(1)}, u32[]{:S(2)}, u32[]{:S(2)}) %collective-permute-start.5) | collective-permute-done | bytes 196640 | tf_op jit(solution)/shard_map/ppermute | solution.py:21
  27.9 0.7 fusion.4
  28.6 0.8 fusion.13
  29.4 0.4 fusion.16
  29.9 0.7 fusion.6
  30.5 0.8 fusion.10
  31.6 0.4 fusion.77
  31.9 1.2 %collective-permute-start.9 = (bf16[768,256]{1,0:T(8,128)(2,1)S(1)}, bf16[768,256]{1,0:T(8,128)(2,1)S(1)}, u32[]{:S(2)}, u32[]{:S(2)}) collective-permute-start(bf16[768,256]{1,0:T(8,128)(2,1)S(1)} %get-tuple-element.71), channel_id=1, source_target_pairs={{0,2},{1,3},{2,0},{3,1},{4,6},{5,7},{6,4},{7,5},{8,10},{9,11},{10,... | collective-permute-start | bytes 1179656 | tf_op jit(solution)/shard_map/ppermute | solution.py:21
  33.1 10.1 %collective-permute-done.9 = bf16[768,256]{1,0:T(8,128)(2,1)S(1)} collective-permute-done((bf16[768,256]{1,0:T(8,128)(2,1)S(1)}, bf16[768,256]{1,0:T(8,128)(2,1)S(1)}, u32[]{:S(2)}, u32[]{:S(2)}) %collective-permute-start.9) | collective-permute-done | bytes 393248 | tf_op jit(solution)/shard_map/ppermute | solution.py:21
  43.4 1.2 %multiply_convert_fusion.1 = (bf16[384,256]{1,0:T(8,128)(2,1)S(1)}, f32[384,256]{1,0:T(8,128)S(1)}, bf16[384,256]{1,0:T(8,128)(2,1)}) fusion(f32[384]{0:T(512)S(1)} %get-tuple-element.70, bf16[384,256]{1,0:T(8,128)(2,1)S(1)} %copy-done.1, f32[256]{0:T(256)S(1)} %copy-done.2, f32[384,256]{1,0:T(8,128)S(1)} %get-tuple-element.65.refs_0_, ...), kind=kOutput, calls=%fused_computation.66 | convolution fusion | flops 303464448 | bytes 1509888 | tf_op jit(solution)/shard_map/dot_general | solution.py:480
  44.6 0.5 multiply_convert_fusion
  45.0 1.1 %weight_blocks.1 = f32[2,80,256]{2,1,0:T(8,128)S(1)} custom-call(f32[384,256]{1,0:T(8,128)S(1)} %get-tuple-element.65.refs_0_, f32[384,256]{1,0:T(8,128)S(1)} %get-tuple-element.64.refs_1_, bf16[384,256]{1,0:T(8,128)(2,1)S(1)} %get-tuple-element.44.refs_2_.refs_6_, bf16[384,256]{1,0:T(8,128)(2,1)S(1)} %get-tuple-element.45.refs_3_, ...), custom_call_target="tpu_custom_call" | custom-call | flops 603979776 | bytes 3145728 | tf_op jit(solution)/shard_map/weight_blocks/pallas_call | solution.py:345
  46.2 0.5 collective-permute-start.10
  46.7 0.6 fusion.38
  47.5 0.6 convolution_add_fusion.1
  48.1 0.6 collective-permute-done.12.refs_1_
  48.7 3.4 %collective-permute-start.13 = (f32[80,256]{1,0:T(8,128)S(1)}, f32[80,256]{1,0:T(8,128)S(1)}, u32[]{:S(2)}, u32[]{:S(2)}) collective-permute-start(f32[80,256]{1,0:T(8,128)S(1)} %build_message.4.refs_1_), channel_id=1, source_target_pairs={{0,16},{4,20},{8,24},{12,28},{16,0},{20,4},{24,8},{28,12},{1,17},{... | collective-permute-start | bytes 245768 | tf_op jit(solution)/shard_map/ppermute | solution.py:21
  53.3 1.5 %collective-permute-start.16 = (bf16[384,256]{1,0:T(8,128)(2,1)S(1)}, bf16[384,256]{1,0:T(8,128)(2,1)S(1)}, u32[]{:S(2)}, u32[]{:S(2)}) collective-permute-start(bf16[384,256]{1,0:T(8,128)(2,1)S(1)} %fusion.47), channel_id=1, source_target_pairs={{0,8},{4,12},{8,0},{12,4},{16,24},{20,28},{24,16},{28,20},{1,9},{5... | collective-permute-start | bytes 589832 | tf_op jit(solution)/shard_map/ppermute | solution.py:21
  54.8 1.5 %collective-permute-start.14 = (bf16[384,256]{1,0:T(8,128)(2,1)S(1)}, bf16[384,256]{1,0:T(8,128)(2,1)S(1)}, u32[]{:S(2)}, u32[]{:S(2)}) collective-permute-start(bf16[384,256]{1,0:T(8,128)(2,1)S(1)} %fusion.46), channel_id=1, source_target_pairs={{0,4},{4,0},{8,12},{12,8},{16,20},{20,16},{24,28},{28,24},{1,5},{5... | collective-permute-start | bytes 589832 | tf_op jit(solution)/shard_map/ppermute | solution.py:21
  56.3 0.6 fusion.40
  57.3 0.6 convolution_add_fusion
  58.2 0.7 collective-permute-start.18
  59.8 1.4 %collective-permute-done.16 = bf16[384,256]{1,0:T(8,128)(2,1)S(1)} collective-permute-done((bf16[384,256]{1,0:T(8,128)(2,1)S(1)}, bf16[384,256]{1,0:T(8,128)(2,1)S(1)}, u32[]{:S(2)}, u32[]{:S(2)}) %collective-permute-start.16) | collective-permute-done | bytes 196640 | tf_op jit(solution)/shard_map/ppermute | solution.py:21
  61.5 1.6 %collective-permute-start.17 = (bf16[384,256]{1,0:T(8,128)(2,1)S(1)}, bf16[384,256]{1,0:T(8,128)(2,1)S(1)}, u32[]{:S(2)}, u32[]{:S(2)}) collective-permute-start(bf16[384,256]{1,0:T(8,128)(2,1)S(1)} %fusion.43), channel_id=1, source_target_pairs={{0,4},{4,0},{8,12},{12,8},{16,20},{20,16},{24,28},{28,24},{1,5},{5... | collective-permute-start | bytes 589832 | tf_op jit(solution)/shard_map/ppermute | solution.py:21
  63.4 1.5 %collective-permute-start.15 = (bf16[384,256]{1,0:T(8,128)(2,1)S(1)}, bf16[384,256]{1,0:T(8,128)(2,1)S(1)}, u32[]{:S(2)}, u32[]{:S(2)}) collective-permute-start(bf16[384,256]{1,0:T(8,128)(2,1)S(1)} %fusion.45), channel_id=1, source_target_pairs={{0,8},{4,12},{8,0},{12,4},{16,24},{20,28},{24,16},{28,20},{1,9},{5... | collective-permute-start | bytes 589832 | tf_op jit(solution)/shard_map/ppermute | solution.py:21
  64.9 1.7 %collective-permute-done.18.refs_2_ = bf16[464,256]{1,0:T(8,128)(2,1)S(1)} collective-permute-done((bf16[464,256]{1,0:T(8,128)(2,1)S(1)}, bf16[464,256]{1,0:T(8,128)(2,1)S(1)}, u32[]{:S(2)}, u32[]{:S(2)}) %collective-permute-start.18) | collective-permute-done | bytes 237600 | tf_op jit(solution)/shard_map/ppermute | solution.py:21
  66.6 1.1 %collective-permute-done.17 = bf16[384,256]{1,0:T(8,128)(2,1)S(1)} collective-permute-done((bf16[384,256]{1,0:T(8,128)(2,1)S(1)}, bf16[384,256]{1,0:T(8,128)(2,1)S(1)}, u32[]{:S(2)}, u32[]{:S(2)}) %collective-permute-start.17) | collective-permute-done | bytes 196640 | tf_op jit(solution)/shard_map/ppermute | solution.py:21
  68.7 1.0 %collective-permute-start.20 = (bf16[384,256]{1,0:T(8,128)(2,1)S(1)}, bf16[384,256]{1,0:T(8,128)(2,1)S(1)}, u32[]{:S(2)}, u32[]{:S(2)}) collective-permute-start(bf16[384,256]{1,0:T(8,128)(2,1)S(1)} %fusion.42), channel_id=1, source_target_pairs={{0,16},{4,20},{8,24},{12,28},{16,0},{20,4},{24,8},{28,12},{1,17},{... | collective-permute-start | bytes 589832 | tf_op jit(solution)/shard_map/ppermute | solution.py:21
  69.7 1.6 %collective-permute-start.19 = (bf16[464,256]{1,0:T(8,128)(2,1)S(1)}, bf16[464,256]{1,0:T(8,128)(2,1)S(1)}, u32[]{:S(2)}, u32[]{:S(2)}) collective-permute-start(bf16[464,256]{1,0:T(8,128)(2,1)S(1)} %build_message.6.refs_0_), channel_id=1, source_target_pairs={{0,4},{4,0},{8,12},{12,8},{16,20},{20,16},{24,28},{28,24},{1,5},{5... | collective-permute-start | bytes 712712 | tf_op jit(solution)/shard_map/ppermute | solution.py:21
  71.6 4.3 %collective-permute-done.19.refs_1_ = bf16[464,256]{1,0:T(8,128)(2,1)S(1)} collective-permute-done((bf16[464,256]{1,0:T(8,128)(2,1)S(1)}, bf16[464,256]{1,0:T(8,128)(2,1)S(1)}, u32[]{:S(2)}, u32[]{:S(2)}) %collective-permute-start.19) | collective-permute-done | bytes 237600 | tf_op jit(solution)/shard_map/ppermute | solution.py:21
  76.0 1.6 %collective-permute-start.22 = (bf16[80,256]{1,0:T(8,128)(2,1)S(1)}, bf16[80,256]{1,0:T(8,128)(2,1)S(1)}, u32[]{:S(2)}, u32[]{:S(2)}) collective-permute-start(bf16[80,256]{1,0:T(8,128)(2,1)S(1)} %build_message.7.refs_0_), channel_id=1, source_target_pairs={{0,2},{1,3},{2,0},{3,1},{4,6},{5,7},{6,4},{7,5},{8,10},{9,11},{10,... | collective-permute-start | bytes 122888 | tf_op jit(solution)/shard_map/ppermute | solution.py:21
  77.8 0.8 collective-permute-done.20
  78.6 0.4 fusion.44
  79.0 0.9 %convolution_convert_fusion = bf16[384,256]{1,0:T(8,128)(2,1)} fusion(bf16[384,256]{1,0:T(8,128)(2,1)S(1)} %fusion.44, bf16[256,256]{1,0:T(8,128)(2,1)S(1)} %copy-done), kind=kOutput, calls=%fused_computation.58 | convolution fusion | flops 50429952 | bytes 524288 | tf_op jit(solution)/shard_map/dot_general | solution.py:537
  79.9 0.4 collective-permute-done.22.refs_2_
  80.4 0.7 join_blocks.1
  (50 shorter events, 5.8 us)
Async XLA Ops:
  0.6 42.7 %copy-start = (bf16[256,256]{1,0:T(8,128)(2,1)S(1)}, bf16[256,256]{1,0:T(8,128)(2,1)}, u32[]{:S(2)}) copy-start(bf16[256,256]{1,0:T(8,128)(2,1)} %param.10) | copy-start | bytes 393220
  2.5 13.9 %collective-permute-start.1 = (bf16[384,256]{1,0:T(8,128)(2,1)S(1)}, bf16[384,256]{1,0:T(8,128)(2,1)S(1)}, u32[]{:S(2)}, u32[]{:S(2)}) collective-permute-start(bf16[384,256]{1,0:T(8,128)(2,1)S(1)} %multiply_convert_fusion.3), channel_id=1, source_target_pairs={{0,16},{4,20},{8,24},{12,28},{16,0},{20,4},{24,8},{28,12},{1,17},{... | collective-permute-start | bytes 589832 | tf_op jit(solution)/shard_map/ppermute | solution.py:21
  6.6 9.8 %collective-permute-start = (bf16[384,256]{1,0:T(8,128)(2,1)S(1)}, bf16[384,256]{1,0:T(8,128)(2,1)S(1)}, u32[]{:S(2)}, u32[]{:S(2)}) collective-permute-start(bf16[384,256]{1,0:T(8,128)(2,1)S(1)} %multiply_convert_fusion.3), channel_id=1, source_target_pairs={{0,8},{4,12},{8,0},{12,4},{16,24},{20,28},{24,16},{28,20},{1,9},{5... | collective-permute-start | bytes 589832 | tf_op jit(solution)/shard_map/ppermute | solution.py:21
  8.2 8.3 %collective-permute-start.2 = (bf16[384,256]{1,0:T(8,128)(2,1)}, bf16[384,256]{1,0:T(8,128)(2,1)S(1)}, u32[]{:S(2)}, u32[]{:S(2)}) collective-permute-start(bf16[384,256]{1,0:T(8,128)(2,1)} %param.17), channel_id=1, source_target_pairs={{0,2},{1,3},{2,0},{3,1},{4,6},{5,7},{6,4},{7,5},{8,10},{9,11},{10,... | collective-permute-start | bytes 589832 | tf_op jit(solution)/shard_map/ppermute | solution.py:21
  9.7 9.4 %collective-permute-start.4 = (bf16[384,256]{1,0:T(8,128)(2,1)S(1)}, bf16[384,256]{1,0:T(8,128)(2,1)S(1)}, u32[]{:S(2)}, u32[]{:S(2)}) collective-permute-start(bf16[384,256]{1,0:T(8,128)(2,1)S(1)} %multiply_convert_fusion.3), channel_id=1, source_target_pairs={{0,4},{4,0},{8,12},{12,8},{16,20},{20,16},{24,28},{28,24},{1,5},{5... | collective-permute-start | bytes 589832 | tf_op jit(solution)/shard_map/ppermute | solution.py:21
  16.5 5.7 %collective-permute-start.3 = (bf16[384,256]{1,0:T(8,128)(2,1)S(1)}, bf16[384,256]{1,0:T(8,128)(2,1)S(1)}, u32[]{:S(2)}, u32[]{:S(2)}) collective-permute-start(bf16[384,256]{1,0:T(8,128)(2,1)S(1)} %collective-permute-done.1), channel_id=1, source_target_pairs={{0,8},{4,12},{8,0},{12,4},{16,24},{20,28},{24,16},{28,20},{1,9},{5... | collective-permute-start | bytes 589832 | tf_op jit(solution)/shard_map/ppermute | solution.py:21
  17.5 5.8 %collective-permute-start.6 = (bf16[384,256]{1,0:T(8,128)(2,1)S(1)}, bf16[384,256]{1,0:T(8,128)(2,1)S(1)}, u32[]{:S(2)}, u32[]{:S(2)}) collective-permute-start(bf16[384,256]{1,0:T(8,128)(2,1)S(1)} %collective-permute-done.1), channel_id=1, source_target_pairs={{0,4},{4,0},{8,12},{12,8},{16,20},{20,16},{24,28},{28,24},{1,5},{5... | collective-permute-start | bytes 589832 | tf_op jit(solution)/shard_map/ppermute | solution.py:21
  22.2 5.7 %collective-permute-start.5 = (bf16[384,256]{1,0:T(8,128)(2,1)S(1)}, bf16[384,256]{1,0:T(8,128)(2,1)S(1)}, u32[]{:S(2)}, u32[]{:S(2)}) collective-permute-start(bf16[384,256]{1,0:T(8,128)(2,1)S(1)} %collective-permute-done.4), channel_id=1, source_target_pairs={{0,8},{4,12},{8,0},{12,4},{16,24},{20,28},{24,16},{28,20},{1,9},{5... | collective-permute-start | bytes 589832 | tf_op jit(solution)/shard_map/ppermute | solution.py:21
  23.3 6.1 %collective-permute-start.7 = (bf16[384,256]{1,0:T(8,128)(2,1)S(1)}, bf16[384,256]{1,0:T(8,128)(2,1)S(1)}, u32[]{:S(2)}, u32[]{:S(2)}) collective-permute-start(bf16[384,256]{1,0:T(8,128)(2,1)S(1)} %collective-permute-done.3), channel_id=1, source_target_pairs={{0,4},{4,0},{8,12},{12,8},{16,20},{20,16},{24,28},{28,24},{1,5},{5... | collective-permute-start | bytes 589832 | tf_op jit(solution)/shard_map/ppermute | solution.py:21
  29.4 14.0 %copy-start.1 = (bf16[384,256]{1,0:T(8,128)(2,1)S(1)}, bf16[384,256]{1,0:T(8,128)(2,1)}, u32[]{:S(2)}) copy-start(bf16[384,256]{1,0:T(8,128)(2,1)} %param.17) | copy-start | bytes 589828
  29.4 14.0 %copy-start.2 = (f32[256]{0:T(256)S(1)}, f32[256]{0:T(256)}, u32[]{:S(2)}) copy-start(f32[256]{0:T(256)} %param.11) | copy-start | bytes 3076
  29.8 1.8 %collective-permute-start.8 = (bf16[768,256]{1,0:T(8,128)(2,1)S(1)}, bf16[768,256]{1,0:T(8,128)(2,1)S(1)}, u32[]{:S(2)}, u32[]{:S(2)}) collective-permute-start(bf16[768,256]{1,0:T(8,128)(2,1)S(1)} %fusion.16), channel_id=1, source_target_pairs={{0,1},{1,0},{2,3},{3,2},{4,5},{5,4},{6,7},{7,6},{8,9},{9,8},{10,11... | collective-permute-start | bytes 1179656 | tf_op jit(solution)/shard_map/ppermute | solution.py:21
  31.9 11.4 %collective-permute-start.9 = (bf16[768,256]{1,0:T(8,128)(2,1)S(1)}, bf16[768,256]{1,0:T(8,128)(2,1)S(1)}, u32[]{:S(2)}, u32[]{:S(2)}) collective-permute-start(bf16[768,256]{1,0:T(8,128)(2,1)S(1)} %get-tuple-element.71), channel_id=1, source_target_pairs={{0,2},{1,3},{2,0},{3,1},{4,6},{5,7},{6,4},{7,5},{8,10},{9,11},{10,... | collective-permute-start | bytes 1179656 | tf_op jit(solution)/shard_map/ppermute | solution.py:21
  46.1 6.0 %collective-permute-start.11 = (bf16[384,256]{1,0:T(8,128)(2,1)S(1)}, bf16[384,256]{1,0:T(8,128)(2,1)S(1)}, u32[]{:S(2)}, u32[]{:S(2)}) collective-permute-start(bf16[384,256]{1,0:T(8,128)(2,1)S(1)} %get-tuple-element.45.refs_3_), channel_id=1, source_target_pairs={{0,1},{1,0},{2,3},{3,2},{4,5},{5,4},{6,7},{7,6},{8,9},{9,8},{10,11... | collective-permute-start | bytes 589832 | tf_op jit(solution)/shard_map/ppermute | solution.py:21
  46.2 5.9 %collective-permute-start.10 = (bf16[384,256]{1,0:T(8,128)(2,1)S(1)}, bf16[384,256]{1,0:T(8,128)(2,1)S(1)}, u32[]{:S(2)}, u32[]{:S(2)}) collective-permute-start(bf16[384,256]{1,0:T(8,128)(2,1)S(1)} %get-tuple-element.44.refs_2_.refs_6_), channel_id=1, source_target_pairs={{0,1},{1,0},{2,3},{3,2},{4,5},{5,4},{6,7},{7,6},{8,9},{9,8},{10,11... | collective-permute-start | bytes 589832 | tf_op jit(solution)/shard_map/ppermute | solution.py:21
  47.3 1.3 %collective-permute-start.12 = (f32[80,256]{1,0:T(8,128)S(1)}, f32[80,256]{1,0:T(8,128)S(1)}, u32[]{:S(2)}, u32[]{:S(2)}) collective-permute-start(f32[80,256]{1,0:T(8,128)S(1)} %get-tuple-element.67), channel_id=1, source_target_pairs={{0,1},{1,0},{2,3},{3,2},{4,5},{5,4},{6,7},{7,6},{8,9},{9,8},{10,11... | collective-permute-start | bytes 245768 | tf_op jit(solution)/shard_map/ppermute | solution.py:21
  48.7 9.5 %collective-permute-start.13 = (f32[80,256]{1,0:T(8,128)S(1)}, f32[80,256]{1,0:T(8,128)S(1)}, u32[]{:S(2)}, u32[]{:S(2)}) collective-permute-start(f32[80,256]{1,0:T(8,128)S(1)} %build_message.4.refs_1_), channel_id=1, source_target_pairs={{0,16},{4,20},{8,24},{12,28},{16,0},{20,4},{24,8},{28,12},{1,17},{... | collective-permute-start | bytes 245768 | tf_op jit(solution)/shard_map/ppermute | solution.py:21
  53.3 7.9 %collective-permute-start.16 = (bf16[384,256]{1,0:T(8,128)(2,1)S(1)}, bf16[384,256]{1,0:T(8,128)(2,1)S(1)}, u32[]{:S(2)}, u32[]{:S(2)}) collective-permute-start(bf16[384,256]{1,0:T(8,128)(2,1)S(1)} %fusion.47), channel_id=1, source_target_pairs={{0,8},{4,12},{8,0},{12,4},{16,24},{20,28},{24,16},{28,20},{1,9},{5... | collective-permute-start | bytes 589832 | tf_op jit(solution)/shard_map/ppermute | solution.py:21
  54.8 6.7 %collective-permute-start.14 = (bf16[384,256]{1,0:T(8,128)(2,1)S(1)}, bf16[384,256]{1,0:T(8,128)(2,1)S(1)}, u32[]{:S(2)}, u32[]{:S(2)}) collective-permute-start(bf16[384,256]{1,0:T(8,128)(2,1)S(1)} %fusion.46), channel_id=1, source_target_pairs={{0,4},{4,0},{8,12},{12,8},{16,20},{20,16},{24,28},{28,24},{1,5},{5... | collective-permute-start | bytes 589832 | tf_op jit(solution)/shard_map/ppermute | solution.py:21
  58.2 8.3 %collective-permute-start.18 = (bf16[464,256]{1,0:T(8,128)(2,1)S(1)}, bf16[464,256]{1,0:T(8,128)(2,1)S(1)}, u32[]{:S(2)}, u32[]{:S(2)}) collective-permute-start(bf16[464,256]{1,0:T(8,128)(2,1)S(1)} %build_message.5.refs_1_), channel_id=1, source_target_pairs={{0,8},{4,12},{8,0},{12,4},{16,24},{20,28},{24,16},{28,20},{1,9},{5... | collective-permute-start | bytes 712712 | tf_op jit(solution)/shard_map/ppermute | solution.py:21
  61.5 6.2 %collective-permute-start.17 = (bf16[384,256]{1,0:T(8,128)(2,1)S(1)}, bf16[384,256]{1,0:T(8,128)(2,1)S(1)}, u32[]{:S(2)}, u32[]{:S(2)}) collective-permute-start(bf16[384,256]{1,0:T(8,128)(2,1)S(1)} %fusion.43), channel_id=1, source_target_pairs={{0,4},{4,0},{8,12},{12,8},{16,20},{20,16},{24,28},{28,24},{1,5},{5... | collective-permute-start | bytes 589832 | tf_op jit(solution)/shard_map/ppermute | solution.py:21
  63.4 14.4 %collective-permute-start.15 = (bf16[384,256]{1,0:T(8,128)(2,1)S(1)}, bf16[384,256]{1,0:T(8,128)(2,1)S(1)}, u32[]{:S(2)}, u32[]{:S(2)}) collective-permute-start(bf16[384,256]{1,0:T(8,128)(2,1)S(1)} %fusion.45), channel_id=1, source_target_pairs={{0,8},{4,12},{8,0},{12,4},{16,24},{20,28},{24,16},{28,20},{1,9},{5... | collective-permute-start | bytes 589832 | tf_op jit(solution)/shard_map/ppermute | solution.py:21
  68.7 9.9 %collective-permute-start.20 = (bf16[384,256]{1,0:T(8,128)(2,1)S(1)}, bf16[384,256]{1,0:T(8,128)(2,1)S(1)}, u32[]{:S(2)}, u32[]{:S(2)}) collective-permute-start(bf16[384,256]{1,0:T(8,128)(2,1)S(1)} %fusion.42), channel_id=1, source_target_pairs={{0,16},{4,20},{8,24},{12,28},{16,0},{20,4},{24,8},{28,12},{1,17},{... | collective-permute-start | bytes 589832 | tf_op jit(solution)/shard_map/ppermute | solution.py:21
  69.7 6.2 %collective-permute-start.19 = (bf16[464,256]{1,0:T(8,128)(2,1)S(1)}, bf16[464,256]{1,0:T(8,128)(2,1)S(1)}, u32[]{:S(2)}, u32[]{:S(2)}) collective-permute-start(bf16[464,256]{1,0:T(8,128)(2,1)S(1)} %build_message.6.refs_0_), channel_id=1, source_target_pairs={{0,4},{4,0},{8,12},{12,8},{16,20},{20,16},{24,28},{28,24},{1,5},{5... | collective-permute-start | bytes 712712 | tf_op jit(solution)/shard_map/ppermute | solution.py:21
  75.9 4.0 %collective-permute-start.23 = (bf16[80,256]{1,0:T(8,128)(2,1)S(1)}, bf16[80,256]{1,0:T(8,128)(2,1)S(1)}, u32[]{:S(2)}, u32[]{:S(2)}) collective-permute-start(bf16[80,256]{1,0:T(8,128)(2,1)S(1)} %build_message.7.refs_0_), channel_id=1, source_target_pairs={{0,3},{1,2},{2,1},{3,0},{4,7},{5,6},{6,5},{7,4},{8,11},{9,10},{10,... | collective-permute-start | bytes 122888 | tf_op jit(solution)/shard_map/ppermute | solution.py:21
  76.0 4.4 %collective-permute-start.22 = (bf16[80,256]{1,0:T(8,128)(2,1)S(1)}, bf16[80,256]{1,0:T(8,128)(2,1)S(1)}, u32[]{:S(2)}, u32[]{:S(2)}) collective-permute-start(bf16[80,256]{1,0:T(8,128)(2,1)S(1)} %build_message.7.refs_0_), channel_id=1, source_target_pairs={{0,2},{1,3},{2,0},{3,1},{4,6},{5,7},{6,4},{7,5},{8,10},{9,11},{10,... | collective-permute-start | bytes 122888 | tf_op jit(solution)/shard_map/ppermute | solution.py:21
  77.5 2.8 %collective-permute-start.21 = (bf16[80,256]{1,0:T(8,128)(2,1)S(1)}, bf16[80,256]{1,0:T(8,128)(2,1)S(1)}, u32[]{:S(2)}, u32[]{:S(2)}) collective-permute-start(bf16[80,256]{1,0:T(8,128)(2,1)S(1)} %build_message.7.refs_0_), channel_id=1, source_target_pairs={{0,1},{1,0},{2,3},{3,2},{4,5},{5,4},{6,7},{7,6},{8,9},{9,8},{10,11... | collective-permute-start | bytes 122888 | tf_op jit(solution)/shard_map/ppermute | solution.py:21

commit v2 on v1

--- a/solution.py
+++ b/solution.py
@@ -282,9 +282,10 @@
     near4 = block(4, sent6)
     near4 = message(near4 + moved5.astype(f32) + moved6[:nodes].astype(f32))
     moved4 = swap(near4, "row", 4)
-    near2 = message(block(2, sent6) + moved3.astype(f32))
+    far1 = block(1, sent6)
+    near2 = message(block(2, far1) + moved3.astype(f32))
     moved2 = swap(near2, "row", 2)
-    sent1 = build_message([block(1, near4)], sent6, moved6, width_rows)
+    sent1 = build_message([after(far1, near4)], sent6, moved6, width_rows)
     moved1 = swap(sent1, "row", 1)
     payload = build_message([], sent1, moved1, width_rows)
     total = block(0, near2) + own.astype(f32) + moved2.astype(f32) + moved1[:nodes].astype(f32)

time: 81.3 us -> 81.3 us (level)
  transfers between devices with their start and end apart: 24 -> 24, of which waited for: 11 -> 12; matrix products, arithmetic and copies ran while one was open for 14% -> 14% of each run, Pallas kernels for 6% -> 6%
where the time goes in v2:
time: 81.3 us; the launch traced here: 81.1 us
  starting transfers between devices  31.2 us (38%)
  waiting for transfers between devices  26.2 us (32%)
  matrix products  13.5 us (17%)
  Pallas kernels  6.5 us (8%)
  other arithmetic  1.86 us (2%)
  between operations  1.68 us (2%)
    ppermute x24, starting transfers between devices, swap(): return lax.ppermute(value, axis, [(i, i ^ distance) for i in range(size)])  31.2 us
    ppermute x24, waiting for transfers between devices, swap(): return lax.ppermute(value, axis, [(i, i ^ distance) for i in range(size)])  26.2 us
    dot_general x20, matrix products, transposed(): lax.dot_general(matrix, value, (((0,), (0,)), ((), ())), preferred_elemen...  7.34 us
    pallas_call x1, Pallas kernels, dense_adjacency(): pl.pallas_call(functools.partial(dense_kernel, row_tiles=row_tiles, col_t...  4.57 us
  transfers between devices with their start and end apart: 24, of which 12 were waited for; matrix products, arithmetic and copies ran while one was open for 14% of the time, Pallas kernels for 6%

profile of v2, /device:TPU:0, one launch (start us, length us, event | category | flops | bytes accessed | tf_op | source)
XLA Modules:
  0.0 81.1 jit_solution(5532390786597545010)
XLA Ops:
  0.7 0.7 convert_rsqrt_fusion
  1.5 1.0 %multiply_convert_fusion.3 = bf16[384,256]{1,0:T(8,128)(2,1)S(1)} fusion(bf16[384,256]{1,0:T(8,128)(2,1)} %param.9, f32[384]{0:T(512)S(1)} %get-tuple-element.72), kind=kLoop, calls=%fused_computation.70 | loop fusion | flops 294912 | bytes 394752 | tf_op jit(solution)/shard_map/convert_element_type | solution.py:441
  2.5 4.1 %collective-permute-start.1 = (bf16[384,256]{1,0:T(8,128)(2,1)S(1)}, bf16[384,256]{1,0:T(8,128)(2,1)S(1)}, u32[]{:S(2)}, u32[]{:S(2)}) collective-permute-start(bf16[384,256]{1,0:T(8,128)(2,1)S(1)} %multiply_convert_fusion.3), channel_id=1, source_target_pairs={{0,16},{4,20},{8,24},{12,28},{16,0},{20,4},{24,8},{28,12},{1,17},{... | collective-permute-start | bytes 589832 | tf_op jit(solution)/shard_map/ppermute | solution.py:21
  6.6 1.6 %collective-permute-start = (bf16[384,256]{1,0:T(8,128)(2,1)S(1)}, bf16[384,256]{1,0:T(8,128)(2,1)S(1)}, u32[]{:S(2)}, u32[]{:S(2)}) collective-permute-start(bf16[384,256]{1,0:T(8,128)(2,1)S(1)} %multiply_convert_fusion.3), channel_id=1, source_target_pairs={{0,8},{4,12},{8,0},{12,4},{16,24},{20,28},{24,16},{28,20},{1,9},{5... | collective-permute-start | bytes 589832 | tf_op jit(solution)/shard_map/ppermute | solution.py:21
  8.2 1.5 %collective-permute-start.2 = (bf16[384,256]{1,0:T(8,128)(2,1)}, bf16[384,256]{1,0:T(8,128)(2,1)S(1)}, u32[]{:S(2)}, u32[]{:S(2)}) collective-permute-start(bf16[384,256]{1,0:T(8,128)(2,1)} %param.17), channel_id=1, source_target_pairs={{0,2},{1,3},{2,0},{3,1},{4,6},{5,7},{6,4},{7,5},{8,10},{9,11},{10,... | collective-permute-start | bytes 589832 | tf_op jit(solution)/shard_map/ppermute | solution.py:21
  9.7 1.5 %collective-permute-start.4 = (bf16[384,256]{1,0:T(8,128)(2,1)S(1)}, bf16[384,256]{1,0:T(8,128)(2,1)S(1)}, u32[]{:S(2)}, u32[]{:S(2)}) collective-permute-start(bf16[384,256]{1,0:T(8,128)(2,1)S(1)} %multiply_convert_fusion.3), channel_id=1, source_target_pairs={{0,4},{4,0},{8,12},{12,8},{16,20},{20,16},{24,28},{28,24},{1,5},{5... | collective-permute-start | bytes 589832 | tf_op jit(solution)/shard_map/ppermute | solution.py:21
  11.9 4.6 %dense_adjacency.1 = bf16[3200,1536]{1,0:T(8,128)(2,1)S(1)} custom-call(s32[1,1,176]{2,1,0:T(1,128)} %rows_hbm, s32[1,1,176]{2,1,0:T(1,128)} %cols_hbm.1, s32[1,1]{1,0:T(1,128)S(6)} %copy.15.live_ref, s32[176,128,128]{2,1,0:T(8,128)} %bitcast.36), custom_call_target="tpu_custom_call" | custom-call | flops 4915200 | bytes 11534336 | tf_op jit(solution)/shard_map/dense_adjacency/pallas_call | solution.py:141
  16.5 1.1 %collective-permute-start.3 = (bf16[384,256]{1,0:T(8,128)(2,1)S(1)}, bf16[384,256]{1,0:T(8,128)(2,1)S(1)}, u32[]{:S(2)}, u32[]{:S(2)}) collective-permute-start(bf16[384,256]{1,0:T(8,128)(2,1)S(1)} %collective-permute-done.1), channel_id=1, source_target_pairs={{0,8},{4,12},{8,0},{12,4},{16,24},{20,28},{24,16},{28,20},{1,9},{5... | collective-permute-start | bytes 589832 | tf_op jit(solution)/shard_map/ppermute | solution.py:21
  17.5 1.5 %collective-permute-start.6 = (bf16[384,256]{1,0:T(8,128)(2,1)S(1)}, bf16[384,256]{1,0:T(8,128)(2,1)S(1)}, u32[]{:S(2)}, u32[]{:S(2)}) collective-permute-start(bf16[384,256]{1,0:T(8,128)(2,1)S(1)} %collective-permute-done.1), channel_id=1, source_target_pairs={{0,4},{4,0},{8,12},{12,8},{16,20},{20,16},{24,28},{28,24},{1,5},{5... | collective-permute-start | bytes 589832 | tf_op jit(solution)/shard_map/ppermute | solution.py:21
  19.1 3.2 %collective-permute-done.3 = bf16[384,256]{1,0:T(8,128)(2,1)S(1)} collective-permute-done((bf16[384,256]{1,0:T(8,128)(2,1)S(1)}, bf16[384,256]{1,0:T(8,128)(2,1)S(1)}, u32[]{:S(2)}, u32[]{:S(2)}) %collective-permute-start.3) | collective-permute-done | bytes 196640 | tf_op jit(solution)/shard_map/ppermute | solution.py:21
  22.2 1.1 %collective-permute-start.5 = (bf16[384,256]{1,0:T(8,128)(2,1)S(1)}, bf16[384,256]{1,0:T(8,128)(2,1)S(1)}, u32[]{:S(2)}, u32[]{:S(2)}) collective-permute-start(bf16[384,256]{1,0:T(8,128)(2,1)S(1)} %collective-permute-done.4), channel_id=1, source_target_pairs={{0,8},{4,12},{8,0},{12,4},{16,24},{20,28},{24,16},{28,20},{1,9},{5... | collective-permute-start | bytes 589832 | tf_op jit(solution)/shard_map/ppermute | solution.py:21
  23.3 1.6 %collective-permute-start.7 = (bf16[384,256]{1,0:T(8,128)(2,1)S(1)}, bf16[384,256]{1,0:T(8,128)(2,1)S(1)}, u32[]{:S(2)}, u32[]{:S(2)}) collective-permute-start(bf16[384,256]{1,0:T(8,128)(2,1)S(1)} %collective-permute-done.3), channel_id=1, source_target_pairs={{0,4},{4,0},{8,12},{12,8},{16,20},{20,16},{24,28},{28,24},{1,5},{5... | collective-permute-start | bytes 589832 | tf_op jit(solution)/shard_map/ppermute | solution.py:21
  24.9 3.0 %collective-permute-done.5 = bf16[384,256]{1,0:T(8,128)(2,1)S(1)} collective-permute-done((bf16[384,256]{1,0:T(8,128)(2,1)S(1)}, bf16[384,256]{1,0:T(8,128)(2,1)S(1)}, u32[]{:S(2)}, u32[]{:S(2)}) %collective-permute-start.5) | collective-permute-done | bytes 196640 | tf_op jit(solution)/shard_map/ppermute | solution.py:21
  27.9 0.7 fusion.4
  28.6 0.8 fusion.13
  29.4 0.4 fusion.16
  29.9 0.7 fusion.6
  30.5 0.8 fusion.10
  31.6 0.4 fusion.77
  31.9 1.2 %collective-permute-start.9 = (bf16[768,256]{1,0:T(8,128)(2,1)S(1)}, bf16[768,256]{1,0:T(8,128)(2,1)S(1)}, u32[]{:S(2)}, u32[]{:S(2)}) collective-permute-start(bf16[768,256]{1,0:T(8,128)(2,1)S(1)} %get-tuple-element.73), channel_id=1, source_target_pairs={{0,2},{1,3},{2,0},{3,1},{4,6},{5,7},{6,4},{7,5},{8,10},{9,11},{10,... | collective-permute-start | bytes 1179656 | tf_op jit(solution)/shard_map/ppermute | solution.py:21
  33.1 10.1 %collective-permute-done.9 = bf16[768,256]{1,0:T(8,128)(2,1)S(1)} collective-permute-done((bf16[768,256]{1,0:T(8,128)(2,1)S(1)}, bf16[768,256]{1,0:T(8,128)(2,1)S(1)}, u32[]{:S(2)}, u32[]{:S(2)}) %collective-permute-start.9) | collective-permute-done | bytes 393248 | tf_op jit(solution)/shard_map/ppermute | solution.py:21
  43.4 1.2 %multiply_convert_fusion.1 = (bf16[384,256]{1,0:T(8,128)(2,1)S(1)}, f32[384,256]{1,0:T(8,128)S(1)}, bf16[384,256]{1,0:T(8,128)(2,1)}) fusion(f32[384]{0:T(512)S(1)} %get-tuple-element.72, bf16[384,256]{1,0:T(8,128)(2,1)S(1)} %copy-done.1, f32[256]{0:T(256)S(1)} %copy-done.2, f32[384,256]{1,0:T(8,128)S(1)} %get-tuple-element.67.refs_0_, ...), kind=kOutput, calls=%fused_computation.66 | convolution fusion | flops 303464448 | bytes 1509888 | tf_op jit(solution)/shard_map/dot_general | solution.py:481
  44.6 0.5 multiply_convert_fusion
  45.0 1.1 %weight_blocks.1 = f32[2,80,256]{2,1,0:T(8,128)S(1)} custom-call(f32[384,256]{1,0:T(8,128)S(1)} %get-tuple-element.67.refs_0_, f32[384,256]{1,0:T(8,128)S(1)} %get-tuple-element.66.refs_1_, bf16[384,256]{1,0:T(8,128)(2,1)S(1)} %get-tuple-element.45.refs_2_.refs_6_, bf16[384,256]{1,0:T(8,128)(2,1)S(1)} %get-tuple-element.46.refs_3_, ...), custom_call_target="tpu_custom_call" | custom-call | flops 603979776 | bytes 3145728 | tf_op jit(solution)/shard_map/weight_blocks/pallas_call | solution.py:346
  46.2 0.5 collective-permute-start.10
  46.7 0.6 fusion.38
  47.5 0.6 convolution_add_fusion.1
  48.1 0.6 collective-permute-done.12.refs_1_
  48.7 3.4 %collective-permute-start.13 = (f32[80,256]{1,0:T(8,128)S(1)}, f32[80,256]{1,0:T(8,128)S(1)}, u32[]{:S(2)}, u32[]{:S(2)}) collective-permute-start(f32[80,256]{1,0:T(8,128)S(1)} %build_message.4.refs_1_), channel_id=1, source_target_pairs={{0,16},{4,20},{8,24},{12,28},{16,0},{20,4},{24,8},{28,12},{1,17},{... | collective-permute-start | bytes 245768 | tf_op jit(solution)/shard_map/ppermute | solution.py:21
  53.3 1.5 %collective-permute-start.16 = (bf16[384,256]{1,0:T(8,128)(2,1)S(1)}, bf16[384,256]{1,0:T(8,128)(2,1)S(1)}, u32[]{:S(2)}, u32[]{:S(2)}) collective-permute-start(bf16[384,256]{1,0:T(8,128)(2,1)S(1)} %fusion.47), channel_id=1, source_target_pairs={{0,8},{4,12},{8,0},{12,4},{16,24},{20,28},{24,16},{28,20},{1,9},{5... | collective-permute-start | bytes 589832 | tf_op jit(solution)/shard_map/ppermute | solution.py:21
  54.8 1.5 %collective-permute-start.14 = (bf16[384,256]{1,0:T(8,128)(2,1)S(1)}, bf16[384,256]{1,0:T(8,128)(2,1)S(1)}, u32[]{:S(2)}, u32[]{:S(2)}) collective-permute-start(bf16[384,256]{1,0:T(8,128)(2,1)S(1)} %fusion.46), channel_id=1, source_target_pairs={{0,4},{4,0},{8,12},{12,8},{16,20},{20,16},{24,28},{28,24},{1,5},{5... | collective-permute-start | bytes 589832 | tf_op jit(solution)/shard_map/ppermute | solution.py:21
  56.3 0.6 fusion.40
  57.3 0.6 convolution_add_fusion
  58.2 0.7 collective-permute-start.18
  60.4 0.7 collective-permute-done.16
  61.5 1.6 %collective-permute-start.17 = (bf16[384,256]{1,0:T(8,128)(2,1)S(1)}, bf16[384,256]{1,0:T(8,128)(2,1)S(1)}, u32[]{:S(2)}, u32[]{:S(2)}) collective-permute-start(bf16[384,256]{1,0:T(8,128)(2,1)S(1)} %fusion.43), channel_id=1, source_target_pairs={{0,4},{4,0},{8,12},{12,8},{16,20},{20,16},{24,28},{28,24},{1,5},{5... | collective-permute-start | bytes 589832 | tf_op jit(solution)/shard_map/ppermute | solution.py:21
  63.4 1.5 %collective-permute-start.15 = (bf16[384,256]{1,0:T(8,128)(2,1)S(1)}, bf16[384,256]{1,0:T(8,128)(2,1)S(1)}, u32[]{:S(2)}, u32[]{:S(2)}) collective-permute-start(bf16[384,256]{1,0:T(8,128)(2,1)S(1)} %fusion.45), channel_id=1, source_target_pairs={{0,8},{4,12},{8,0},{12,4},{16,24},{20,28},{24,16},{28,20},{1,9},{5... | collective-permute-start | bytes 589832 | tf_op jit(solution)/shard_map/ppermute | solution.py:21
  64.9 1.7 %collective-permute-done.18.refs_2_ = bf16[464,256]{1,0:T(8,128)(2,1)S(1)} collective-permute-done((bf16[464,256]{1,0:T(8,128)(2,1)S(1)}, bf16[464,256]{1,0:T(8,128)(2,1)S(1)}, u32[]{:S(2)}, u32[]{:S(2)}) %collective-permute-start.18) | collective-permute-done | bytes 237600 | tf_op jit(solution)/shard_map/ppermute | solution.py:21
  66.6 1.1 %collective-permute-done.17 = bf16[384,256]{1,0:T(8,128)(2,1)S(1)} collective-permute-done((bf16[384,256]{1,0:T(8,128)(2,1)S(1)}, bf16[384,256]{1,0:T(8,128)(2,1)S(1)}, u32[]{:S(2)}, u32[]{:S(2)}) %collective-permute-start.17) | collective-permute-done | bytes 196640 | tf_op jit(solution)/shard_map/ppermute | solution.py:21
  68.0 1.6 %collective-permute-start.20 = (bf16[384,256]{1,0:T(8,128)(2,1)S(1)}, bf16[384,256]{1,0:T(8,128)(2,1)S(1)}, u32[]{:S(2)}, u32[]{:S(2)}) collective-permute-start(bf16[384,256]{1,0:T(8,128)(2,1)S(1)} %fusion.42), channel_id=1, source_target_pairs={{0,16},{4,20},{8,24},{12,28},{16,0},{20,4},{24,8},{28,12},{1,17},{... | collective-permute-start | bytes 589832 | tf_op jit(solution)/shard_map/ppermute | solution.py:21
  69.7 1.6 %collective-permute-start.19 = (bf16[464,256]{1,0:T(8,128)(2,1)S(1)}, bf16[464,256]{1,0:T(8,128)(2,1)S(1)}, u32[]{:S(2)}, u32[]{:S(2)}) collective-permute-start(bf16[464,256]{1,0:T(8,128)(2,1)S(1)} %build_message.6.refs_0_), channel_id=1, source_target_pairs={{0,4},{4,0},{8,12},{12,8},{16,20},{20,16},{24,28},{28,24},{1,5},{5... | collective-permute-start | bytes 712712 | tf_op jit(solution)/shard_map/ppermute | solution.py:21
  71.6 4.3 %collective-permute-done.19.refs_1_ = bf16[464,256]{1,0:T(8,128)(2,1)S(1)} collective-permute-done((bf16[464,256]{1,0:T(8,128)(2,1)S(1)}, bf16[464,256]{1,0:T(8,128)(2,1)S(1)}, u32[]{:S(2)}, u32[]{:S(2)}) %collective-permute-start.19) | collective-permute-done | bytes 237600 | tf_op jit(solution)/shard_map/ppermute | solution.py:21
  76.0 1.6 %collective-permute-start.22 = (bf16[80,256]{1,0:T(8,128)(2,1)S(1)}, bf16[80,256]{1,0:T(8,128)(2,1)S(1)}, u32[]{:S(2)}, u32[]{:S(2)}) collective-permute-start(bf16[80,256]{1,0:T(8,128)(2,1)S(1)} %build_message.7.refs_0_), channel_id=1, source_target_pairs={{0,2},{1,3},{2,0},{3,1},{4,6},{5,7},{6,4},{7,5},{8,10},{9,11},{10,... | collective-permute-start | bytes 122888 | tf_op jit(solution)/shard_map/ppermute | solution.py:21
  77.8 0.3 collective-permute-done.20
  78.2 0.4 fusion.44
  78.6 0.9 %convolution_convert_fusion = bf16[384,256]{1,0:T(8,128)(2,1)} fusion(bf16[384,256]{1,0:T(8,128)(2,1)S(1)} %fusion.44, bf16[256,256]{1,0:T(8,128)(2,1)S(1)} %copy-done), kind=kOutput, calls=%fused_computation.58 | convolution fusion | flops 50429952 | bytes 524288 | tf_op jit(solution)/shard_map/dot_general | solution.py:538
  79.8 0.6 collective-permute-done.22.refs_2_
  80.4 0.7 join_blocks.1
  (50 shorter events, 6.1 us)
Async XLA Ops:
  0.6 42.7 %copy-start = (bf16[256,256]{1,0:T(8,128)(2,1)S(1)}, bf16[256,256]{1,0:T(8,128)(2,1)}, u32[]{:S(2)}) copy-start(bf16[256,256]{1,0:T(8,128)(2,1)} %param.10) | copy-start | bytes 393220
  2.5 13.9 %collective-permute-start.1 = (bf16[384,256]{1,0:T(8,128)(2,1)S(1)}, bf16[384,256]{1,0:T(8,128)(2,1)S(1)}, u32[]{:S(2)}, u32[]{:S(2)}) collective-permute-start(bf16[384,256]{1,0:T(8,128)(2,1)S(1)} %multiply_convert_fusion.3), channel_id=1, source_target_pairs={{0,16},{4,20},{8,24},{12,28},{16,0},{20,4},{24,8},{28,12},{1,17},{... | collective-permute-start | bytes 589832 | tf_op jit(solution)/shard_map/ppermute | solution.py:21
  6.6 9.8 %collective-permute-start = (bf16[384,256]{1,0:T(8,128)(2,1)S(1)}, bf16[384,256]{1,0:T(8,128)(2,1)S(1)}, u32[]{:S(2)}, u32[]{:S(2)}) collective-permute-start(bf16[384,256]{1,0:T(8,128)(2,1)S(1)} %multiply_convert_fusion.3), channel_id=1, source_target_pairs={{0,8},{4,12},{8,0},{12,4},{16,24},{20,28},{24,16},{28,20},{1,9},{5... | collective-permute-start | bytes 589832 | tf_op jit(solution)/shard_map/ppermute | solution.py:21
  8.2 8.3 %collective-permute-start.2 = (bf16[384,256]{1,0:T(8,128)(2,1)}, bf16[384,256]{1,0:T(8,128)(2,1)S(1)}, u32[]{:S(2)}, u32[]{:S(2)}) collective-permute-start(bf16[384,256]{1,0:T(8,128)(2,1)} %param.17), channel_id=1, source_target_pairs={{0,2},{1,3},{2,0},{3,1},{4,6},{5,7},{6,4},{7,5},{8,10},{9,11},{10,... | collective-permute-start | bytes 589832 | tf_op jit(solution)/shard_map/ppermute | solution.py:21
  9.7 9.4 %collective-permute-start.4 = (bf16[384,256]{1,0:T(8,128)(2,1)S(1)}, bf16[384,256]{1,0:T(8,128)(2,1)S(1)}, u32[]{:S(2)}, u32[]{:S(2)}) collective-permute-start(bf16[384,256]{1,0:T(8,128)(2,1)S(1)} %multiply_convert_fusion.3), channel_id=1, source_target_pairs={{0,4},{4,0},{8,12},{12,8},{16,20},{20,16},{24,28},{28,24},{1,5},{5... | collective-permute-start | bytes 589832 | tf_op jit(solution)/shard_map/ppermute | solution.py:21
  16.5 5.7 %collective-permute-start.3 = (bf16[384,256]{1,0:T(8,128)(2,1)S(1)}, bf16[384,256]{1,0:T(8,128)(2,1)S(1)}, u32[]{:S(2)}, u32[]{:S(2)}) collective-permute-start(bf16[384,256]{1,0:T(8,128)(2,1)S(1)} %collective-permute-done.1), channel_id=1, source_target_pairs={{0,8},{4,12},{8,0},{12,4},{16,24},{20,28},{24,16},{28,20},{1,9},{5... | collective-permute-start | bytes 589832 | tf_op jit(solution)/shard_map/ppermute | solution.py:21
  17.5 5.8 %collective-permute-start.6 = (bf16[384,256]{1,0:T(8,128)(2,1)S(1)}, bf16[384,256]{1,0:T(8,128)(2,1)S(1)}, u32[]{:S(2)}, u32[]{:S(2)}) collective-permute-start(bf16[384,256]{1,0:T(8,128)(2,1)S(1)} %collective-permute-done.1), channel_id=1, source_target_pairs={{0,4},{4,0},{8,12},{12,8},{16,20},{20,16},{24,28},{28,24},{1,5},{5... | collective-permute-start | bytes 589832 | tf_op jit(solution)/shard_map/ppermute | solution.py:21
  22.2 5.7 %collective-permute-start.5 = (bf16[384,256]{1,0:T(8,128)(2,1)S(1)}, bf16[384,256]{1,0:T(8,128)(2,1)S(1)}, u32[]{:S(2)}, u32[]{:S(2)}) collective-permute-start(bf16[384,256]{1,0:T(8,128)(2,1)S(1)} %collective-permute-done.4), channel_id=1, source_target_pairs={{0,8},{4,12},{8,0},{12,4},{16,24},{20,28},{24,16},{28,20},{1,9},{5... | collective-permute-start | bytes 589832 | tf_op jit(solution)/shard_map/ppermute | solution.py:21
  23.3 6.1 %collective-permute-start.7 = (bf16[384,256]{1,0:T(8,128)(2,1)S(1)}, bf16[384,256]{1,0:T(8,128)(2,1)S(1)}, u32[]{:S(2)}, u32[]{:S(2)}) collective-permute-start(bf16[384,256]{1,0:T(8,128)(2,1)S(1)} %collective-permute-done.3), channel_id=1, source_target_pairs={{0,4},{4,0},{8,12},{12,8},{16,20},{20,16},{24,28},{28,24},{1,5},{5... | collective-permute-start | bytes 589832 | tf_op jit(solution)/shard_map/ppermute | solution.py:21
  29.4 14.0 %copy-start.1 = (bf16[384,256]{1,0:T(8,128)(2,1)S(1)}, bf16[384,256]{1,0:T(8,128)(2,1)}, u32[]{:S(2)}) copy-start(bf16[384,256]{1,0:T(8,128)(2,1)} %param.17) | copy-start | bytes 589828
  29.4 14.0 %copy-start.2 = (f32[256]{0:T(256)S(1)}, f32[256]{0:T(256)}, u32[]{:S(2)}) copy-start(f32[256]{0:T(256)} %param.11) | copy-start | bytes 3076
  29.8 1.8 %collective-permute-start.8 = (bf16[768,256]{1,0:T(8,128)(2,1)S(1)}, bf16[768,256]{1,0:T(8,128)(2,1)S(1)}, u32[]{:S(2)}, u32[]{:S(2)}) collective-permute-start(bf16[768,256]{1,0:T(8,128)(2,1)S(1)} %fusion.16), channel_id=1, source_target_pairs={{0,1},{1,0},{2,3},{3,2},{4,5},{5,4},{6,7},{7,6},{8,9},{9,8},{10,11... | collective-permute-start | bytes 1179656 | tf_op jit(solution)/shard_map/ppermute | solution.py:21
  31.9 11.4 %collective-permute-start.9 = (bf16[768,256]{1,0:T(8,128)(2,1)S(1)}, bf16[768,256]{1,0:T(8,128)(2,1)S(1)}, u32[]{:S(2)}, u32[]{:S(2)}) collective-permute-start(bf16[768,256]{1,0:T(8,128)(2,1)S(1)} %get-tuple-element.73), channel_id=1, source_target_pairs={{0,2},{1,3},{2,0},{3,1},{4,6},{5,7},{6,4},{7,5},{8,10},{9,11},{10,... | collective-permute-start | bytes 1179656 | tf_op jit(solution)/shard_map/ppermute | solution.py:21
  46.1 6.0 %collective-permute-start.11 = (bf16[384,256]{1,0:T(8,128)(2,1)S(1)}, bf16[384,256]{1,0:T(8,128)(2,1)S(1)}, u32[]{:S(2)}, u32[]{:S(2)}) collective-permute-start(bf16[384,256]{1,0:T(8,128)(2,1)S(1)} %get-tuple-element.46.refs_3_), channel_id=1, source_target_pairs={{0,1},{1,0},{2,3},{3,2},{4,5},{5,4},{6,7},{7,6},{8,9},{9,8},{10,11... | collective-permute-start | bytes 589832 | tf_op jit(solution)/shard_map/ppermute | solution.py:21
  46.2 5.9 %collective-permute-start.10 = (bf16[384,256]{1,0:T(8,128)(2,1)S(1)}, bf16[384,256]{1,0:T(8,128)(2,1)S(1)}, u32[]{:S(2)}, u32[]{:S(2)}) collective-permute-start(bf16[384,256]{1,0:T(8,128)(2,1)S(1)} %get-tuple-element.45.refs_2_.refs_6_), channel_id=1, source_target_pairs={{0,1},{1,0},{2,3},{3,2},{4,5},{5,4},{6,7},{7,6},{8,9},{9,8},{10,11... | collective-permute-start | bytes 589832 | tf_op jit(solution)/shard_map/ppermute | solution.py:21
  47.3 1.3 %collective-permute-start.12 = (f32[80,256]{1,0:T(8,128)S(1)}, f32[80,256]{1,0:T(8,128)S(1)}, u32[]{:S(2)}, u32[]{:S(2)}) collective-permute-start(f32[80,256]{1,0:T(8,128)S(1)} %get-tuple-element.69), channel_id=1, source_target_pairs={{0,1},{1,0},{2,3},{3,2},{4,5},{5,4},{6,7},{7,6},{8,9},{9,8},{10,11... | collective-permute-start | bytes 245768 | tf_op jit(solution)/shard_map/ppermute | solution.py:21
  48.7 9.5 %collective-permute-start.13 = (f32[80,256]{1,0:T(8,128)S(1)}, f32[80,256]{1,0:T(8,128)S(1)}, u32[]{:S(2)}, u32[]{:S(2)}) collective-permute-start(f32[80,256]{1,0:T(8,128)S(1)} %build_message.4.refs_1_), channel_id=1, source_target_pairs={{0,16},{4,20},{8,24},{12,28},{16,0},{20,4},{24,8},{28,12},{1,17},{... | collective-permute-start | bytes 245768 | tf_op jit(solution)/shard_map/ppermute | solution.py:21
  53.3 7.9 %collective-permute-start.16 = (bf16[384,256]{1,0:T(8,128)(2,1)S(1)}, bf16[384,256]{1,0:T(8,128)(2,1)S(1)}, u32[]{:S(2)}, u32[]{:S(2)}) collective-permute-start(bf16[384,256]{1,0:T(8,128)(2,1)S(1)} %fusion.47), channel_id=1, source_target_pairs={{0,8},{4,12},{8,0},{12,4},{16,24},{20,28},{24,16},{28,20},{1,9},{5... | collective-permute-start | bytes 589832 | tf_op jit(solution)/shard_map/ppermute | solution.py:21
  54.8 6.7 %collective-permute-start.14 = (bf16[384,256]{1,0:T(8,128)(2,1)S(1)}, bf16[384,256]{1,0:T(8,128)(2,1)S(1)}, u32[]{:S(2)}, u32[]{:S(2)}) collective-permute-start(bf16[384,256]{1,0:T(8,128)(2,1)S(1)} %fusion.46), channel_id=1, source_target_pairs={{0,4},{4,0},{8,12},{12,8},{16,20},{20,16},{24,28},{28,24},{1,5},{5... | collective-permute-start | bytes 589832 | tf_op jit(solution)/shard_map/ppermute | solution.py:21
  58.2 8.3 %collective-permute-start.18 = (bf16[464,256]{1,0:T(8,128)(2,1)S(1)}, bf16[464,256]{1,0:T(8,128)(2,1)S(1)}, u32[]{:S(2)}, u32[]{:S(2)}) collective-permute-start(bf16[464,256]{1,0:T(8,128)(2,1)S(1)} %build_message.5.refs_1_), channel_id=1, source_target_pairs={{0,8},{4,12},{8,0},{12,4},{16,24},{20,28},{24,16},{28,20},{1,9},{5... | collective-permute-start | bytes 712712 | tf_op jit(solution)/shard_map/ppermute | solution.py:21
  61.5 6.2 %collective-permute-start.17 = (bf16[384,256]{1,0:T(8,128)(2,1)S(1)}, bf16[384,256]{1,0:T(8,128)(2,1)S(1)}, u32[]{:S(2)}, u32[]{:S(2)}) collective-permute-start(bf16[384,256]{1,0:T(8,128)(2,1)S(1)} %fusion.43), channel_id=1, source_target_pairs={{0,4},{4,0},{8,12},{12,8},{16,20},{20,16},{24,28},{28,24},{1,5},{5... | collective-permute-start | bytes 589832 | tf_op jit(solution)/shard_map/ppermute | solution.py:21
  63.4 14.4 %collective-permute-start.15 = (bf16[384,256]{1,0:T(8,128)(2,1)S(1)}, bf16[384,256]{1,0:T(8,128)(2,1)S(1)}, u32[]{:S(2)}, u32[]{:S(2)}) collective-permute-start(bf16[384,256]{1,0:T(8,128)(2,1)S(1)} %fusion.45), channel_id=1, source_target_pairs={{0,8},{4,12},{8,0},{12,4},{16,24},{20,28},{24,16},{28,20},{1,9},{5... | collective-permute-start | bytes 589832 | tf_op jit(solution)/shard_map/ppermute | solution.py:21
  68.0 10.1 %collective-permute-start.20 = (bf16[384,256]{1,0:T(8,128)(2,1)S(1)}, bf16[384,256]{1,0:T(8,128)(2,1)S(1)}, u32[]{:S(2)}, u32[]{:S(2)}) collective-permute-start(bf16[384,256]{1,0:T(8,128)(2,1)S(1)} %fusion.42), channel_id=1, source_target_pairs={{0,16},{4,20},{8,24},{12,28},{16,0},{20,4},{24,8},{28,12},{1,17},{... | collective-permute-start | bytes 589832 | tf_op jit(solution)/shard_map/ppermute | solution.py:21
  69.7 6.2 %collective-permute-start.19 = (bf16[464,256]{1,0:T(8,128)(2,1)S(1)}, bf16[464,256]{1,0:T(8,128)(2,1)S(1)}, u32[]{:S(2)}, u32[]{:S(2)}) collective-permute-start(bf16[464,256]{1,0:T(8,128)(2,1)S(1)} %build_message.6.refs_0_), channel_id=1, source_target_pairs={{0,4},{4,0},{8,12},{12,8},{16,20},{20,16},{24,28},{28,24},{1,5},{5... | collective-permute-start | bytes 712712 | tf_op jit(solution)/shard_map/ppermute | solution.py:21
  75.9 3.9 %collective-permute-start.23 = (bf16[80,256]{1,0:T(8,128)(2,1)S(1)}, bf16[80,256]{1,0:T(8,128)(2,1)S(1)}, u32[]{:S(2)}, u32[]{:S(2)}) collective-permute-start(bf16[80,256]{1,0:T(8,128)(2,1)S(1)} %build_message.7.refs_0_), channel_id=1, source_target_pairs={{0,3},{1,2},{2,1},{3,0},{4,7},{5,6},{6,5},{7,4},{8,11},{9,10},{10,... | collective-permute-start | bytes 122888 | tf_op jit(solution)/shard_map/ppermute | solution.py:21
  76.0 4.4 %collective-permute-start.22 = (bf16[80,256]{1,0:T(8,128)(2,1)S(1)}, bf16[80,256]{1,0:T(8,128)(2,1)S(1)}, u32[]{:S(2)}, u32[]{:S(2)}) collective-permute-start(bf16[80,256]{1,0:T(8,128)(2,1)S(1)} %build_message.7.refs_0_), channel_id=1, source_target_pairs={{0,2},{1,3},{2,0},{3,1},{4,6},{5,7},{6,4},{7,5},{8,10},{9,11},{10,... | collective-permute-start | bytes 122888 | tf_op jit(solution)/shard_map/ppermute | solution.py:21
  77.6 2.8 %collective-permute-start.21 = (bf16[80,256]{1,0:T(8,128)(2,1)S(1)}, bf16[80,256]{1,0:T(8,128)(2,1)S(1)}, u32[]{:S(2)}, u32[]{:S(2)}) collective-permute-start(bf16[80,256]{1,0:T(8,128)(2,1)S(1)} %build_message.7.refs_0_), channel_id=1, source_target_pairs={{0,1},{1,0},{2,3},{3,2},{4,5},{5,4},{6,7},{7,6},{8,9},{9,8},{10,11... | collective-permute-start | bytes 122888 | tf_op jit(solution)/shard_map/ppermute | solution.py:21
